TPU v7x, 256 devices: a whole 4x4x8 slice. The times are simulated.
256 devices in a mesh: section: 2 (over core), group: 32 (over z, y), tp: 4 (over x).
Axes of the slice: x: 4, y: 4, z: 8, core: 2. Of those that a mesh axis runs over, the one named last changes fastest.
Arguments:
- resp_queries: bfloat16 [16384, 5120], P(('section', 'group', 'tp')), may hold values from -8 to 8
- resp_keys: bfloat16 [16384, 1024], P(('section', 'group', 'tp')), may hold values from -6 to 6
- resp_values: bfloat16 [16384, 1024], P(('section', 'group', 'tp')), may hold values from -6 to 6
- resp_dout: bfloat16 [16384, 5120], P(('section', 'group', 'tp')), may hold values from -6 to 6
- prompt_kv: bfloat16 [32, 2, 1024, 1024], P('group', None, None, 'tp'), may hold values from -8 to 8
- lengths: int32 [64], P(('section', 'group')), may hold values from 64 to 256, as said below
- owners: int32 [64], P(('section', 'group')), may hold values from 0 to 3
- visible_tiles: int32 [64, 8], P(('section', 'group')), may hold values from 0 to 1, as said below
Outputs:
- resp_dq: bfloat16 [16384, 5120], P(('section', 'group', 'tp'))
- resp_dk: bfloat16 [16384, 1024], P(('section', 'group', 'tp'))
- resp_dv: bfloat16 [16384, 1024], P(('section', 'group', 'tp'))
- prompt_grads: bfloat16 [32, 2, 1024, 1024], P('group', None, 'section', 'tp')
Inputs may be any that keep to these rules, and one draw needn't show every extreme that they name: Response j lies on section index j // 32 and group index g = j mod 32 and belongs to the prompt on group index (g - owners[j]) mod 32. `lengths`: rows of a response at or past its length are padding; some response fills all 256 slots. `visible_tiles`: tile 0 of a prompt is visible to every response.
All inputs are finite; a program needn't handle non-finite values.
Results may differ from a plain program's by a relative error of at most 0.04.
Values may be sent and summed in bfloat16 or wider, within the bound.
No kernel may reach another device: no remote copies, remote signals or barrier semaphores. Data moves between devices by JAX's collectives and lax.ppermute only.
A program may use at most 128 MiB of HBM per device.

v0:
```python
import jax
import jax.numpy as jnp
from jax import lax
from jax.sharding import PartitionSpec as P

HEADS = 40
KV_HEADS = 8
HEAD_DIM = 128
PTILE = 128
WIN = 4


MASKED = -1e30


def shifted(block, axis, distance):
    devices = range(lax.axis_size(axis))
    route = [((i - distance) % len(devices), i) for i in devices]
    return lax.ppermute(block, axis, route)


def attend_head(queries, keys_head, values_head, grad_out, allowed, live_rows, scaling):
    scores = (
        jnp.einsum("qgd,td->gqt", queries, keys_head, preferred_element_type=jnp.float32) * scaling
    )
    scores = jnp.where(allowed, scores, MASKED)
    largest = jnp.max(scores, axis=-1, keepdims=True)
    exponent = jnp.exp(scores - largest)
    probabilities = exponent / jnp.sum(exponent, axis=-1, keepdims=True)
    probabilities = probabilities * live_rows[:, None]
    weights = probabilities.astype(jnp.bfloat16)
    attended = jnp.einsum(
        "gqt,td->qgd", weights, values_head, preferred_element_type=jnp.float32
    ).astype(jnp.bfloat16)
    row_delta = jnp.sum(grad_out.astype(jnp.float32) * attended.astype(jnp.float32), axis=-1)
    grad_prob = jnp.einsum("qgd,td->gqt", grad_out, values_head, preferred_element_type=jnp.float32)
    grad_scores = (
        probabilities * (grad_prob - jnp.transpose(row_delta, (1, 0))[..., None])
    ).astype(jnp.bfloat16)
    grad_query = (
        jnp.einsum("gqt,td->qgd", grad_scores, keys_head, preferred_element_type=jnp.float32)
        * scaling
    ).astype(jnp.bfloat16)
    grad_key = (
        jnp.einsum("gqt,qgd->td", grad_scores, queries, preferred_element_type=jnp.float32)
        * scaling
    )
    grad_value = jnp.einsum("gqt,qgd->td", weights, grad_out, preferred_element_type=jnp.float32)
    return (grad_query, grad_key, grad_value)


def attend(query_rows, key_rows, value_rows, dout_rows, prompt_tiles, length, visible):
    row_count = query_rows.shape[0]
    prompt_len = prompt_tiles.shape[1]
    kv_count = key_rows.shape[1] // HEAD_DIM
    per_kv = HEADS // KV_HEADS
    scaling = HEAD_DIM ** (-0.5)
    keys_all = jnp.concatenate([prompt_tiles[0], key_rows], 0).reshape(
        prompt_len + row_count, kv_count, HEAD_DIM
    )
    values_all = jnp.concatenate([prompt_tiles[1], value_rows], 0).reshape(
        prompt_len + row_count, kv_count, HEAD_DIM
    )
    queries = query_rows.reshape(row_count, kv_count, per_kv, HEAD_DIM)
    grad_out = dout_rows.reshape(row_count, kv_count, per_kv, HEAD_DIM)
    position = jnp.arange(row_count, dtype=jnp.int32)
    open_prompt = jnp.repeat(visible, PTILE, total_repeat_length=prompt_len) == 1
    causal = position[None, :] <= position[:, None]
    allowed = jnp.concatenate(
        [jnp.broadcast_to(open_prompt[None, :], (row_count, prompt_len)), causal], 1
    )
    live_rows = (position < length).astype(jnp.float32)
    query_heads = []
    key_heads = []
    value_heads = []
    for head in range(kv_count):
        grad_query, grad_key, grad_value = attend_head(
            queries[:, head],
            keys_all[:, head],
            values_all[:, head],
            grad_out[:, head],
            allowed,
            live_rows,
            scaling,
        )
        query_heads.append(grad_query)
        key_heads.append(grad_key)
        value_heads.append(grad_value)
    grad_query = jnp.stack(query_heads, 1).reshape(row_count, -1)
    grad_key = jnp.stack(key_heads, 1)
    grad_value = jnp.stack(value_heads, 1)
    return (grad_query, grad_key, grad_value)


def shards(
    resp_queries, resp_keys, resp_values, resp_dout, prompt_kv, lengths, owners, visible_tiles
):
    queries, keys_local, values_local, grad_rows = (
        lax.all_to_all(resp_queries, "tp", split_axis=1, concat_axis=0, tiled=True),
        lax.all_to_all(resp_keys, "tp", split_axis=1, concat_axis=0, tiled=True),
        lax.all_to_all(resp_values, "tp", split_axis=1, concat_axis=0, tiled=True),
        lax.all_to_all(resp_dout, "tp", split_axis=1, concat_axis=0, tiled=True),
    )
    own_tiles = prompt_kv[0]
    offers = [own_tiles]
    for offset in range(1, WIN):
        offers.append(shifted(own_tiles, "group", offset))
    offered = jnp.stack(offers)
    seq_count = lengths.shape[0]
    resp_len = queries.shape[0] // seq_count
    prompt_len = own_tiles.shape[1]
    columns = own_tiles.shape[2]
    shares = [jnp.zeros(own_tiles.shape, jnp.float32) for offset in range(WIN)]
    chosen = lax.dynamic_index_in_dim(offered, owners[0], 0, keepdims=False)
    grad_query, grad_key, grad_value = attend(
        queries, keys_local, values_local, grad_rows, chosen, lengths[0], visible_tiles[0]
    )
    collected = jnp.stack([grad_key[:prompt_len], grad_value[:prompt_len]]).reshape(
        2, prompt_len, columns
    )
    for offset in range(WIN):
        shares[offset] = jnp.where(owners[0] == offset, collected, 0.0)
    key_parts = grad_key[prompt_len:].reshape(resp_len, columns).astype(jnp.bfloat16)
    value_parts = grad_value[prompt_len:].reshape(resp_len, columns).astype(jnp.bfloat16)
    returned = (
        lax.all_to_all(grad_query, "tp", split_axis=0, concat_axis=1, tiled=True),
        lax.all_to_all(key_parts, "tp", split_axis=0, concat_axis=1, tiled=True),
        lax.all_to_all(value_parts, "tp", split_axis=0, concat_axis=1, tiled=True),
    )
    summed = shares[0]
    for offset in range(1, WIN):
        summed = summed + shifted(shares[offset], "group", -offset)
    reduced = lax.psum_scatter(summed, "section", scatter_dimension=1, tiled=True)
    prompt_grads = reduced.astype(jnp.bfloat16)[None]
    return (returned[0], returned[1], returned[2], prompt_grads)


def solution(mesh):
    placed = (
        P(("section", "group", "tp"), None),
        P(("section", "group", "tp"), None),
        P(("section", "group", "tp"), None),
        P(("section", "group", "tp"), None),
        P("group", None, None, "tp"),
        P(("section", "group")),
        P(("section", "group")),
        P(("section", "group"), None),
    )
    return jax.shard_map(
        shards,
        mesh=mesh,
        in_specs=placed,
        out_specs=(
            P(("section", "group", "tp"), None),
            P(("section", "group", "tp"), None),
            P(("section", "group", "tp"), None),
            P("group", None, "section", "tp"),
        ),
        check_vma=False,
    )
```

profile of v0, /device:TPU:104, one launch (start us, length us, event | category | flops | bytes accessed | tf_op | source)
XLA Modules:
  0.0 398.0 jit_solution(6413790989001944972)
XLA Ops:
  7.2 1.5 copy.73
  8.7 3.1 collective-permute-start.2
  11.8 2.6 collective-permute-start.1
  14.4 1.9 collective-permute-start
  16.3 1.6 copy.180
  17.9 4.3 %all-to-all-start = ((bf16[64,4,256]{2,0,1:T(8,128)(2,1)}), bf16[64,4,256]{2,0,1:T(8,128)(2,1)S(1)}, u32[]{:S(2)}, u32[]{:S(2)}) async-start(bf16[64,4,256]{2,0,1:T(8,128)(2,1)} %bitcast.205), calls=%async_computation | async-start | bytes 262144 | tf_op jit(solution)/shard_map/all_to_all | solution.py:100
  22.2 1.6 copy.179
  24.7 3.5 all-to-all-done
  28.1 3.3 all-to-all-start.2
  31.5 5.9 %all-to-all-done.2 = bf16[64,4,256]{2,0,1:T(8,128)(2,1)S(1)} async-done(((bf16[64,4,256]{2,0,1:T(8,128)(2,1)}), bf16[64,4,256]{2,0,1:T(8,128)(2,1)S(1)}, u32[]{:S(2)}, u32[]{:S(2)}) %all-to-all-start.2) | async-done | bytes 131104 | tf_op jit(solution)/shard_map/all_to_all | solution.py:101
  37.4 3.5 all-to-all-start.1
  42.3 2.0 copy.177
  44.2 4.5 %compare_select_fusion.1 = s32[1024,1]{0,1:T(1,128)S(1)} fusion(s32[]{:T(128)} %bitcast.14, s32[]{:T(128)} %bitcast.15, s32[]{:T(128)} %bitcast.16, s32[]{:T(128)} %bitcast.17, s32[]{:T(128)} %bitcast.18, s32[]{:T(128)} %bitcast.20, s32[]{:T(128)} %bitcast.19, s32[1024,1]{0,1:T(1,128)S(1)} %bitcast.241, s32[1024,1]{0,1:T(1,128)S(1)} %bitcast.239), kind=kLoop, calls=%fused_computation.100 | loop fusion | flops 14336 | bytes 12316 | tf_op jit(solution)/shard_map/jit(_take)/gather | solution.py:67
  49.7 4.5 %all-to-all-start.3 = ((bf16[64,4,1280]{2,0,1:T(8,128)(2,1)}), bf16[64,4,1280]{2,0,1:T(8,128)(2,1)}, u32[]{:S(2)}, u32[]{:S(2)}) async-start(bf16[64,4,1280]{2,0,1:T(8,128)(2,1)} %bitcast.202), calls=%async_computation.3 | async-start | bytes 1310720 | tf_op jit(solution)/shard_map/all_to_all | solution.py:102
  57.3 5.8 %all-to-all-done.3 = bf16[64,4,1280]{2,0,1:T(8,128)(2,1)} async-done(((bf16[64,4,1280]{2,0,1:T(8,128)(2,1)}), bf16[64,4,1280]{2,0,1:T(8,128)(2,1)}, u32[]{:S(2)}, u32[]{:S(2)}) %all-to-all-start.3) | async-done | bytes 655392 | tf_op jit(solution)/shard_map/all_to_all | solution.py:102
  63.0 1.8 reshape.173
  68.8 5.1 %fusion.76 = (f32[5,256]{1,0:T(8,128)S(1)}, f32[5,256,1280]{1,2,0:T(8,128)}) fusion(pred[256,1280]{0,1:T(8,128)(4,1)S(1)} %copy-done.17, bf16[256,1,5,128]{3,2,1,0:T(8,128)(2,1)S(1)} %copy-done.11, bf16[1024,2,128]{2,0,1:T(8,128)(2,1)S(1)} %copy.75, bf16[256,2,128]{2,0,1:T(8,128)(2,1)S(1)} %copy.76), kind=kOutput, calls=%fused_computation.123 | convolution fusion | flops 426640640 | bytes 7869440 | tf_op jit(solution)/shard_map/sub | solution.py:28
  73.9 5.1 %fusion.79 = (f32[5,256]{1,0:T(8,128)S(1)}, f32[5,256,1280]{1,2,0:T(8,128)}) fusion(pred[256,1280]{0,1:T(8,128)(4,1)S(1)} %copy-done.17, bf16[256,1,5,128]{3,2,1,0:T(8,128)(2,1)S(1)} %copy-done.13, bf16[256,2,128]{2,0,1:T(8,128)(2,1)S(1)} %copy.76, bf16[1024,2,128]{2,0,1:T(8,128)(2,1)S(1)} %copy.75), kind=kOutput, calls=%fused_computation.124 | convolution fusion | flops 426640640 | bytes 7869440 | tf_op jit(solution)/shard_map/sub | solution.py:28
  79.0 5.9 %fusion.18 = (bf16[5,256,1280]{1,2,0:T(8,128)(2,1)S(1)}, bf16[5,256,1280]{1,2,0:T(8,128)(2,1)S(1)}) fusion(f32[256]{0:T(256)S(1)} %copy-done.19, f32[5,256,1280]{1,2,0:T(8,128)} %get-tuple-element.36, f32[5,256]{1,0:T(8,128)S(1)} %get-tuple-element.35, f32[5,256,1280]{1,2,0:T(8,128)} %get-tuple-element.38, f32[5,256]{1,0:T(8,128)S(1)} %get-tuple-element.37), kind=kLoop, calls=%fused_computation.34 | loop fusion | flops 9830400 | bytes 19672064 | tf_op jit(solution)/shard_map/convert_element_type | solution.py:31
  84.9 2.1 convolution_bitcast_fusion.1
  87.0 1.6 fusion.28
  88.6 1.6 fusion.29
  90.2 2.1 convolution_bitcast_fusion
  92.3 1.3 fusion.5
  94.6 1.3 fusion.3
  95.9 1.2 fusion.15
  97.3 1.2 fusion.17
  98.6 1.2 pad_maximum_fusion.2
  99.8 2.5 copy.110
  102.3 2.3 pad_maximum_fusion.1
  104.6 2.5 copy.111
  107.1 4.3 %broadcast_select_fusion.2 = (f32[2,1024,256]{2,1,0:T(8,128)}, f32[2,1024,256]{2,1,0:T(8,128)}, f32[2,1024,256]{2,1,0:T(8,128)}) fusion(pred[]{:T(512)S(6)} %eq.21, f32[1,1024,256]{2,1,0:T(8,128)} %copy.111, f32[1,1024,256]{2,1,0:T(8,128)} %copy.110, pred[]{:T(512)S(6)} %eq.22, pred[]{:T(512)S(6)} %eq.23), kind=kLoop, calls=%fused_computation.68 | loop fusion | flops 2097152 | bytes 8388611 | tf_op jit(solution)/shard_map/jit(_where)/select_n | solution.py:122
  111.5 16.2 %collective-permute-start.3 = (f32[2,1024,256]{2,1,0:T(8,128)}, f32[2,1024,256]{2,1,0:T(8,128)}, u32[]{:S(2)}, u32[]{:S(2)}) collective-permute-start(f32[2,1024,256]{2,1,0:T(8,128)} %get-tuple-element.16), channel_id=1, source_target_pairs={{4,0},{8,4},{12,8},{16,12},{20,16},{24,20},{28,24},{32,28},{36,32}... | collective-permute-start | bytes 6291464 | tf_op jit(solution)/shard_map/ppermute | solution.py:19
  128.7 84.1 %collective-permute-done.3 = f32[2,1024,256]{2,1,0:T(8,128)} collective-permute-done((f32[2,1024,256]{2,1,0:T(8,128)}, f32[2,1024,256]{2,1,0:T(8,128)}, u32[]{:S(2)}, u32[]{:S(2)}) %collective-permute-start.3) | collective-permute-done | bytes 2097184 | tf_op jit(solution)/shard_map/ppermute | solution.py:19
  212.8 4.8 %collective-permute-done.4 = f32[2,1024,256]{2,1,0:T(8,128)} collective-permute-done((f32[2,1024,256]{2,1,0:T(8,128)}, f32[2,1024,256]{2,1,0:T(8,128)}, u32[]{:S(2)}, u32[]{:S(2)}) %collective-permute-start.4) | collective-permute-done | bytes 2097184 | tf_op jit(solution)/shard_map/ppermute | solution.py:19
  217.6 128.2 %collective-permute-done.5 = f32[2,1024,256]{2,1,0:T(8,128)} collective-permute-done((f32[2,1024,256]{2,1,0:T(8,128)}, f32[2,1024,256]{2,1,0:T(8,128)}, u32[]{:S(2)}, u32[]{:S(2)}) %collective-permute-start.5) | collective-permute-done | bytes 2097184 | tf_op jit(solution)/shard_map/ppermute | solution.py:19
  345.8 5.3 %add_add_fusion = f32[2,1024,256]{2,1,0:T(8,128)} fusion(f32[2,1024,256]{2,1,0:T(8,128)} %collective-permute-done.5, f32[2,1024,256]{2,1,0:T(8,128)} %collective-permute-done.4, f32[2,1024,256]{2,1,0:T(8,128)} %collective-permute-done.3, pred[]{:T(512)S(6)} %eq.20, f32[1,1024,256]{2,1,0:T(8,128)} %copy.111, f32[1,1024,256]{2,1,0:T(8,128)} %copy.110), kind=kLoop, calls=%fused_computation.37 | loop fusion | flops 2621440 | bytes 10485761 | tf_op jit(solution)/shard_map/add | solution.py:132
  351.1 1.6 fusion.48
  354.5 4.3 %all-to-all-start.5 = ((bf16[4,64,256]{2,1,0:T(8,128)(2,1)}), bf16[4,64,256]{2,1,0:T(8,128)(2,1)S(1)}, u32[]{:S(2)}, u32[]{:S(2)}) async-start(bf16[4,64,256]{2,1,0:T(8,128)(2,1)} %convert_element_type.87), calls=%async_computation.5 | async-start | bytes 262144 | tf_op jit(solution)/shard_map/all_to_all | solution.py:127
  358.8 4.2 %fusion.30 = bf16[256,1,5,128]{0,3,2,1:T(8,128)(2,1)} fusion(bf16[5,256,1280]{1,2,0:T(8,128)(2,1)} %copy-done, bf16[256,2,128]{2,0,1:T(8,128)(2,1)S(1)} %copy.76, bf16[1024,2,128]{2,0,1:T(8,128)(2,1)} %copy-done.5), kind=kOutput, calls=%fused_computation.57 | convolution fusion | flops 420413440 | bytes 4259840 | tf_op jit(solution)/shard_map/gqt,td->qgd/dot_general | solution.py:41
  363.0 1.4 fusion.31
  365.3 4.7 %all-to-all-start.6 = ((bf16[4,64,256]{2,1,0:T(8,128)(2,1)}), bf16[4,64,256]{2,1,0:T(8,128)(2,1)S(1)}, u32[]{:S(2)}, u32[]{:S(2)}) async-start(bf16[4,64,256]{2,1,0:T(8,128)(2,1)} %convert_element_type.88), calls=%async_computation.6 | async-start | bytes 262144 | tf_op jit(solution)/shard_map/all_to_all | solution.py:128
  370.0 1.1 pad_maximum_fusion.3
  372.1 1.6 all_to_all.98
  373.7 2.3 all-to-all-done.6
  375.9 3.5 all-to-all-start.4
  380.8 7.4 %all-to-all-done.4 = bf16[4,64,1280]{2,1,0:T(8,128)(2,1)S(1)} async-done(((bf16[4,64,1280]{2,1,0:T(8,128)(2,1)}), bf16[4,64,1280]{2,1,0:T(8,128)(2,1)S(1)}, u32[]{:S(2)}, u32[]{:S(2)}) %all-to-all-start.4) | async-done | bytes 655392 | tf_op jit(solution)/shard_map/all_to_all | solution.py:126
  389.1 2.1 convert_bitcast_fusion
  (92 shorter events, 17.0 us)
Async XLA Ops:
  7.2 16.6 %copy-start.16 = (bf16[64,5120]{1,0:T(8,128)(2,1)S(1)}, bf16[64,5120]{1,0:T(8,128)(2,1)}, u32[]{:S(2)}) copy-start(bf16[64,5120]{1,0:T(8,128)(2,1)} %param.10) | copy-start | bytes 1966084
  7.2 33.7 %copy-start.18 = (s32[1,8]{1,0:T(1,128)S(1)}, s32[1,8]{1,0:T(1,128)}, u32[]{:S(2)}) copy-start(s32[1,8]{1,0:T(1,128)} %param.17) | copy-start | bytes 100
  8.7 58.1 %collective-permute-start.2 = (bf16[2,1024,256]{1,2,0:T(8,128)(2,1)S(1)}, bf16[2,1024,256]{1,2,0:T(8,128)(2,1)}, u32[]{:S(2)}, u32[]{:S(2)}) collective-permute-start(bf16[2,1024,256]{1,2,0:T(8,128)(2,1)S(1)} %bitcast.220), channel_id=1, source_target_pairs={{116,0},{120,4},{124,8},{0,12},{4,16},{8,20},{12,24},{16,28},{20,3... | collective-permute-start | bytes 3145736 | tf_op jit(solution)/shard_map/ppermute | solution.py:19
  11.8 55.0 %collective-permute-start.1 = (bf16[2,1024,256]{1,2,0:T(8,128)(2,1)S(1)}, bf16[2,1024,256]{1,2,0:T(8,128)(2,1)}, u32[]{:S(2)}, u32[]{:S(2)}) collective-permute-start(bf16[2,1024,256]{1,2,0:T(8,128)(2,1)S(1)} %bitcast.221), channel_id=1, source_target_pairs={{120,0},{124,4},{0,8},{4,12},{8,16},{12,20},{16,24},{20,28},{24,32... | collective-permute-start | bytes 3145736 | tf_op jit(solution)/shard_map/ppermute | solution.py:19
  14.4 52.4 %collective-permute-start = (bf16[2,1024,256]{1,2,0:T(8,128)(2,1)S(1)}, bf16[2,1024,256]{1,2,0:T(8,128)(2,1)}, u32[]{:S(2)}, u32[]{:S(2)}) collective-permute-start(bf16[2,1024,256]{1,2,0:T(8,128)(2,1)S(1)} %bitcast.222), channel_id=1, source_target_pairs={{124,0},{0,4},{4,8},{8,12},{12,16},{16,20},{20,24},{24,28},{28,32}... | collective-permute-start | bytes 3145736 | tf_op jit(solution)/shard_map/ppermute | solution.py:19
  17.9 10.3 %all-to-all-start = ((bf16[64,4,256]{2,0,1:T(8,128)(2,1)}), bf16[64,4,256]{2,0,1:T(8,128)(2,1)S(1)}, u32[]{:S(2)}, u32[]{:S(2)}) async-start(bf16[64,4,256]{2,0,1:T(8,128)(2,1)} %bitcast.205), calls=%async_computation | async-start | bytes 262144 | tf_op jit(solution)/shard_map/all_to_all | solution.py:100
  28.1 9.3 %all-to-all-start.2 = ((bf16[64,4,256]{2,0,1:T(8,128)(2,1)}), bf16[64,4,256]{2,0,1:T(8,128)(2,1)S(1)}, u32[]{:S(2)}, u32[]{:S(2)}) async-start(bf16[64,4,256]{2,0,1:T(8,128)(2,1)} %bitcast.204), calls=%async_computation.2 | async-start | bytes 262144 | tf_op jit(solution)/shard_map/all_to_all | solution.py:101
  37.4 12.2 %all-to-all-start.1 = ((bf16[64,4,1280]{2,0,1:T(8,128)(2,1)}), bf16[64,4,1280]{2,0,1:T(8,128)(2,1)S(1)}, u32[]{:S(2)}, u32[]{:S(2)}) async-start(bf16[64,4,1280]{2,0,1:T(8,128)(2,1)} %bitcast.203), calls=%async_computation.1 | async-start | bytes 1310720 | tf_op jit(solution)/shard_map/all_to_all | solution.py:99
  49.7 13.4 %all-to-all-start.3 = ((bf16[64,4,1280]{2,0,1:T(8,128)(2,1)}), bf16[64,4,1280]{2,0,1:T(8,128)(2,1)}, u32[]{:S(2)}, u32[]{:S(2)}) async-start(bf16[64,4,1280]{2,0,1:T(8,128)(2,1)} %bitcast.202), calls=%async_computation.3 | async-start | bytes 1310720 | tf_op jit(solution)/shard_map/all_to_all | solution.py:102
  54.1 334.9 %reduce-scatter.2.cloned.1.call-start = ((), (), s32[]{:S(2)}) async-start(), calls=%async_computation.8 | async-start | bytes 3145728 | tf_op jit(solution)/shard_map/reduce_scatter | solution.py:133
  66.9 23.3 %copy-start.7 = (bf16[256,1,5,128]{3,2,1,0:T(8,128)(2,1)}, bf16[256,1,5,128]{3,2,1,0:T(8,128)(2,1)S(1)}, u32[]{:S(2)}) copy-start(bf16[256,1,5,128]{3,2,1,0:T(8,128)(2,1)S(1)} %get-tuple-element.20) | copy-start | bytes 983044
  67.7 1.0 copy-start.11
  67.7 1.1 copy-start.17
  68.1 20.5 %copy-start.9 = (bf16[1024,2,128]{2,0,1:T(8,128)(2,1)}, bf16[1024,2,128]{2,0,1:T(8,128)(2,1)S(1)}, u32[]{:S(2)}) copy-start(bf16[1024,2,128]{2,0,1:T(8,128)(2,1)S(1)} %copy.80) | copy-start | bytes 1572868
  68.4 5.5 %copy-start.5 = (bf16[1024,2,128]{2,0,1:T(8,128)(2,1)}, bf16[1024,2,128]{2,0,1:T(8,128)(2,1)S(1)}, u32[]{:S(2)}) copy-start(bf16[1024,2,128]{2,0,1:T(8,128)(2,1)S(1)} %copy.75) | copy-start | bytes 1572868
  68.8 5.1 %copy-start.13 = (bf16[256,1,5,128]{3,2,1,0:T(8,128)(2,1)S(1)}, bf16[256,1,5,128]{3,2,1,0:T(8,128)(2,1)}, u32[]{:S(2)}) copy-start(bf16[256,1,5,128]{3,2,1,0:T(8,128)(2,1)} %get-tuple-element.22) | copy-start | bytes 983044
  73.9 5.1 %copy-start.19 = (f32[256]{0:T(256)S(1)}, f32[256]{0:T(256)}, u32[]{:S(2)}) copy-start(f32[256]{0:T(256)} %compare_convert_fusion) | copy-start | bytes 3076
  79.0 5.9 %copy-start.15 = (bf16[256,1,5,128]{3,2,1,0:T(8,128)(2,1)S(1)}, bf16[256,1,5,128]{3,2,1,0:T(8,128)(2,1)}, u32[]{:S(2)}) copy-start(bf16[256,1,5,128]{3,2,1,0:T(8,128)(2,1)} %get-tuple-element.19) | copy-start | bytes 983044
  87.0 5.3 %slice-start.2 = ((s8[6553600]{0:T(1024)(128)(4,1)}), s8[2359296]{0:T(1024)(128)(4,1)S(1)}, s32[]{:S(2)}) async-start(s8[6553600]{0:T(1024)(128)(4,1)} %bitcast.216), calls=%async_computation.11 | async-start | bytes 4718592
  88.5 3.7 slice-start.3
  88.5 3.7 copy-start.20
  90.1 2.1 copy-start.10
  90.1 3.4 slice-start
  92.3 2.2 slice-start.1
  92.3 2.3 copy-start.8
  94.6 1.3 copy-start.14
  95.9 2.7 copy-start
  95.9 1.4 copy-start.12
  97.3 2.4 copy-start.3
  98.6 1.2 copy-start.4
  111.5 101.3 %collective-permute-start.3 = (f32[2,1024,256]{2,1,0:T(8,128)}, f32[2,1024,256]{2,1,0:T(8,128)}, u32[]{:S(2)}, u32[]{:S(2)}) collective-permute-start(f32[2,1024,256]{2,1,0:T(8,128)} %get-tuple-element.16), channel_id=1, source_target_pairs={{4,0},{8,4},{12,8},{16,12},{20,16},{24,20},{28,24},{32,28},{36,32}... | collective-permute-start | bytes 6291464 | tf_op jit(solution)/shard_map/ppermute | solution.py:19
  127.6 89.9 %collective-permute-start.4 = (f32[2,1024,256]{2,1,0:T(8,128)}, f32[2,1024,256]{2,1,0:T(8,128)}, u32[]{:S(2)}, u32[]{:S(2)}) collective-permute-start(f32[2,1024,256]{2,1,0:T(8,128)} %get-tuple-element.17), channel_id=1, source_target_pairs={{8,0},{12,4},{16,8},{20,12},{24,16},{28,20},{32,24},{36,28},{40,32... | collective-permute-start | bytes 6291464 | tf_op jit(solution)/shard_map/ppermute | solution.py:19
  127.6 218.2 %collective-permute-start.5 = (f32[2,1024,256]{2,1,0:T(8,128)}, f32[2,1024,256]{2,1,0:T(8,128)}, u32[]{:S(2)}, u32[]{:S(2)}) collective-permute-start(f32[2,1024,256]{2,1,0:T(8,128)} %get-tuple-element.18), channel_id=1, source_target_pairs={{12,0},{16,4},{20,8},{24,12},{28,16},{32,20},{36,24},{40,28},{44,3... | collective-permute-start | bytes 6291464 | tf_op jit(solution)/shard_map/ppermute | solution.py:19
  354.5 10.8 %all-to-all-start.5 = ((bf16[4,64,256]{2,1,0:T(8,128)(2,1)}), bf16[4,64,256]{2,1,0:T(8,128)(2,1)S(1)}, u32[]{:S(2)}, u32[]{:S(2)}) async-start(bf16[4,64,256]{2,1,0:T(8,128)(2,1)} %convert_element_type.87), calls=%async_computation.5 | async-start | bytes 262144 | tf_op jit(solution)/shard_map/all_to_all | solution.py:127
  358.8 4.2 %copy-start.6 = (bf16[1024,2,128]{2,0,1:T(8,128)(2,1)S(1)}, bf16[1024,2,128]{2,0,1:T(8,128)(2,1)}, u32[]{:S(2)}) copy-start(bf16[1024,2,128]{2,0,1:T(8,128)(2,1)} %copy-done.5) | copy-start | bytes 1572868
  358.8 5.5 %copy-start.1 = (f32[1280,1,128]{0,2,1:T(8,128)S(1)}, f32[1280,1,128]{0,2,1:T(8,128)}, u32[]{:S(2)}) copy-start(f32[1280,1,128]{0,2,1:T(8,128)} %convolution_bitcast_fusion.1) | copy-start | bytes 1966084
  358.8 5.5 %copy-start.2 = (f32[1280,1,128]{0,2,1:T(8,128)S(1)}, f32[1280,1,128]{0,2,1:T(8,128)}, u32[]{:S(2)}) copy-start(f32[1280,1,128]{0,2,1:T(8,128)} %convolution_bitcast_fusion) | copy-start | bytes 1966084
  365.3 10.7 %all-to-all-start.6 = ((bf16[4,64,256]{2,1,0:T(8,128)(2,1)}), bf16[4,64,256]{2,1,0:T(8,128)(2,1)S(1)}, u32[]{:S(2)}, u32[]{:S(2)}) async-start(bf16[4,64,256]{2,1,0:T(8,128)(2,1)} %convert_element_type.88), calls=%async_computation.6 | async-start | bytes 262144 | tf_op jit(solution)/shard_map/all_to_all | solution.py:128
  375.9 12.2 %all-to-all-start.4 = ((bf16[4,64,1280]{2,1,0:T(8,128)(2,1)}), bf16[4,64,1280]{2,1,0:T(8,128)(2,1)S(1)}, u32[]{:S(2)}, u32[]{:S(2)}) async-start(bf16[4,64,1280]{2,1,0:T(8,128)(2,1)} %all_to_all.98), calls=%async_computation.4 | async-start | bytes 1310720 | tf_op jit(solution)/shard_map/all_to_all | solution.py:126
Sparse Core Ops, SparseCore 0:
  351.2 12.6 reduce-scatter.1
where the time goes:
time: 399 us; the launch traced here: 398 us
  waiting for transfers between devices  242 us (61%)
  starting transfers between devices  52.9 us (13%)
  other arithmetic  31.4 us (8%)
  matrix products  28 us (7%)
  local copies, waits for them, and re-layouts  27.7 us (7%)
  between operations  15.7 us (4%)
    ppermute x6, waiting for transfers between devices, shifted(): return lax.ppermute(block, axis, route)  217 us
    ppermute x6, starting transfers between devices, shifted(): return lax.ppermute(block, axis, route)  24.8 us
    sub x2, matrix products, attend_head(): exponent = jnp.exp(scores - largest)  10.1 us
  transfers between devices with their start and end apart: 14, of which 9 were waited for; matrix products, arithmetic and copies ran while one was open for 8% of the time, Pallas kernels for 0%

commit v1 on v0

v1 whole, which is shorter than its diff:
```python
import functools

import jax
import jax.numpy as jnp
from jax import lax
from jax.experimental import pallas as pl
from jax.experimental.pallas import tpu as pltpu
from jax.sharding import PartitionSpec as P

HEADS = 40
KV_HEADS = 8
HEAD_DIM = 128
PTILE = 128
WIN = 4
PER_KV = HEADS // KV_HEADS
CHUNKS = 1

MASKED = -1e30
SCALING = HEAD_DIM ** (-0.5)
LOG2E = 1.4426950408889634
VMEM_LIMIT = 48 * 1024 * 1024

TP, SECTION, LENGTH, VISIBLE = 0, 1, 2, 3


def shifted(block, axis, distance):
    devices = range(lax.axis_size(axis))
    route = [((i - distance) % len(devices), i) for i in devices]
    return lax.ppermute(block, axis, route)


def whole():
    return pl.BlockSpec(memory_space=pltpu.VMEM)


def scalars():
    return pl.BlockSpec(memory_space=pltpu.SMEM)


def pack_kernel(tp_count, meta, queries, grad_out, keys, values, *packs):
    q_cols = queries.shape[1] // tp_count
    k_cols = keys.shape[1] // tp_count
    q_part, k_part = q_cols // CHUNKS, k_cols // CHUNKS
    for chunk in range(CHUNKS):
        for d in range(tp_count):
            owner = lax.rem(meta[TP] + d, tp_count)
            pack = packs[chunk * tp_count + d]
            q_at = pl.ds(pl.multiple_of(owner * q_cols + chunk * q_part, 128), q_part)
            k_at = pl.ds(pl.multiple_of(owner * k_cols + chunk * k_part, 128), k_part)
            pack[:, :q_part] = queries[:, q_at]
            pack[:, q_part : 2 * q_part] = grad_out[:, q_at]
            pack[:, 2 * q_part : 2 * q_part + k_part] = keys[:, k_at]
            pack[:, 2 * q_part + k_part :] = values[:, k_at]


def unpack_kernel(tp_count, meta, *refs):
    packs, (grad_q, grad_k, grad_v) = refs[:-3], refs[-3:]
    q_cols = grad_q.shape[1] // tp_count
    k_cols = grad_k.shape[1] // tp_count
    q_part, k_part = q_cols // CHUNKS, k_cols // CHUNKS
    for chunk in range(CHUNKS):
        for d in range(tp_count):
            owner = lax.rem(meta[TP] + d, tp_count)
            pack = packs[chunk * tp_count + d]
            q_at = pl.ds(pl.multiple_of(owner * q_cols + chunk * q_part, 128), q_part)
            k_at = pl.ds(pl.multiple_of(owner * k_cols + chunk * k_part, 128), k_part)
            grad_q[:, q_at] = pack[:, :q_part]
            grad_k[:, k_at] = pack[:, q_part : q_part + k_part]
            grad_v[:, k_at] = pack[:, q_part + k_part :]


def place(index, tp, tp_count, rows):
    block = index // rows
    return lax.rem(tp - block + tp_count, tp_count) * rows + lax.rem(index, rows)


def attend_kernel(tp_count, kv_heads, meta, *refs):
    packs = refs[:tp_count]
    own, other = refs[tp_count : tp_count + 2]
    backs = refs[tp_count + 2 : 2 * tp_count + 2]
    own_grad, other_grad = refs[2 * tp_count + 2 : 2 * tp_count + 4]
    q_all, do_all, keys, values, keys_t, bias, scores, grad_prob, weights, grad_scores, dk, dv = refs[
        2 * tp_count + 4 :
    ]
    rows = packs[0].shape[0]
    resp = rows * tp_count
    half = own.shape[1]
    prompt_len = 2 * half
    total = prompt_len + resp
    per_half = half // PTILE
    q_cols = kv_heads * PER_KV * HEAD_DIM
    k_cols = kv_heads * HEAD_DIM
    tp, section, length = meta[TP], meta[SECTION], meta[LENGTH]

    key_at = place(lax.broadcasted_iota(jnp.int32, (resp, resp), 0), tp, tp_count, rows)
    row_at = place(lax.broadcasted_iota(jnp.int32, (resp, resp), 1), tp, tp_count, rows)
    bias[...] = jnp.where(key_at <= row_at, 0.0, MASKED)
    live = (
        place(lax.broadcasted_iota(jnp.int32, (1, resp), 1), tp, tp_count, rows) < length
    ).astype(jnp.float32)
    tile_bias = []
    for tile in range(2 * per_half):
        side = section if tile < per_half else 1 - section
        visible = meta[VISIBLE + side * per_half + tile % per_half]
        tile_bias.append(jnp.where(visible == 1, 0.0, MASKED))

    nt = (((1,), (1,)), ((), ()))
    for kv in range(kv_heads):
        at = slice(kv * HEAD_DIM, (kv + 1) * HEAD_DIM)
        keys[:half] = own[0, :, at]
        keys[half:prompt_len] = other[0, :, at]
        values[:half] = own[1, :, at]
        values[half:prompt_len] = other[1, :, at]
        for d in range(tp_count):
            pack = packs[d]
            k_from = 2 * q_cols + kv * HEAD_DIM
            keys[prompt_len + d * rows : prompt_len + (d + 1) * rows] = pack[
                :, k_from : k_from + HEAD_DIM
            ]
            v_from = k_from + k_cols
            values[prompt_len + d * rows : prompt_len + (d + 1) * rows] = pack[
                :, v_from : v_from + HEAD_DIM
            ]
            for head in range(PER_KV):
                q_from = (kv * PER_KV + head) * HEAD_DIM
                q_all[head, d * rows : (d + 1) * rows] = pack[:, q_from : q_from + HEAD_DIM]
                do_all[head, d * rows : (d + 1) * rows] = pack[
                    :, q_cols + q_from : q_cols + q_from + HEAD_DIM
                ]
        keys_t[...] = keys[...].T
        dk[...] = jnp.zeros_like(dk)
        dv[...] = jnp.zeros_like(dv)

        for head in range(PER_KV):
            query = q_all[head]
            cotangent = do_all[head]
            tops = []
            for tile in range(total // PTILE):
                span = slice(tile * PTILE, (tile + 1) * PTILE)
                part = lax.dot_general(
                    keys[span], query, nt, preferred_element_type=jnp.float32
                )
                if tile >= 2 * per_half:
                    low = (tile - 2 * per_half) * PTILE
                    part = part + bias[low : low + PTILE]
                scores[span] = part
                top = jnp.max(part.reshape(PTILE // 8, 8, resp), axis=0)
                if tile < 2 * per_half:
                    top = top + tile_bias[tile]
                tops.append(top)
                grad_prob[span] = lax.dot_general(
                    values[span], cotangent, nt, preferred_element_type=jnp.float32
                )
            largest = jnp.max(functools.reduce(jnp.maximum, tops), axis=0, keepdims=True)
            factor = SCALING * LOG2E
            sums = jnp.zeros((8, resp), jnp.float32)
            dots = jnp.zeros((8, resp), jnp.float32)
            for tile in range(total // PTILE):
                span = slice(tile * PTILE, (tile + 1) * PTILE)
                shift = largest
                if tile < 2 * per_half:
                    shift = shift - tile_bias[tile]
                exponent = jnp.exp2((scores[span] - shift) * factor)
                scores[span] = exponent
                sums += jnp.sum(exponent.reshape(PTILE // 8, 8, resp), axis=0)
                dots += jnp.sum((exponent * grad_prob[span]).reshape(PTILE // 8, 8, resp), axis=0)
            inverse = 1.0 / jnp.sum(sums, axis=0, keepdims=True)
            row_delta = jnp.sum(dots, axis=0, keepdims=True) * inverse
            inverse = inverse * live
            for tile in range(total // PTILE):
                span = slice(tile * PTILE, (tile + 1) * PTILE)
                probabilities = scores[span] * inverse
                weights[span] = probabilities.astype(jnp.bfloat16)
                grad_scores[span] = (probabilities * (grad_prob[span] - row_delta)).astype(
                    jnp.bfloat16
                )
            dv[...] += jnp.dot(weights[...], cotangent, preferred_element_type=jnp.float32)
            dk[...] += jnp.dot(grad_scores[...], query, preferred_element_type=jnp.float32)
            grad_query_t = jnp.dot(
                keys_t[...], grad_scores[...], preferred_element_type=jnp.float32
            )
            grad_query = (grad_query_t.T * SCALING).astype(jnp.bfloat16)
            q_from = (kv * PER_KV + head) * HEAD_DIM
            for d in range(tp_count):
                backs[d][:, q_from : q_from + HEAD_DIM] = grad_query[d * rows : (d + 1) * rows]

        own_grad[0, :, at] = (dk[:half] * SCALING).astype(jnp.bfloat16)
        other_grad[0, :, at] = (dk[half:prompt_len] * SCALING).astype(jnp.bfloat16)
        own_grad[1, :, at] = dv[:half].astype(jnp.bfloat16)
        other_grad[1, :, at] = dv[half:prompt_len].astype(jnp.bfloat16)
        for d in range(tp_count):
            k_from = q_cols + kv * HEAD_DIM
            span = slice(prompt_len + d * rows, prompt_len + (d + 1) * rows)
            backs[d][:, k_from : k_from + HEAD_DIM] = (dk[span] * SCALING).astype(jnp.bfloat16)
            backs[d][:, k_from + k_cols : k_from + k_cols + HEAD_DIM] = dv[span].astype(
                jnp.bfloat16
            )


def attend(meta, packs, own, other):
    tp_count = len(packs)
    rows = packs[0].shape[0]
    resp = rows * tp_count
    half, k_cols = own.shape[1:]
    kv_heads = k_cols // HEAD_DIM
    q_cols = kv_heads * PER_KV * HEAD_DIM
    total = 2 * half + resp
    f32, bf16 = jnp.float32, jnp.bfloat16
    flops = 10 * resp * total * kv_heads * PER_KV * HEAD_DIM
    results = pl.pallas_call(
        functools.partial(attend_kernel, tp_count, kv_heads),
        out_shape=[jax.ShapeDtypeStruct((rows, q_cols + 2 * k_cols), bf16)] * tp_count
        + [jax.ShapeDtypeStruct(own.shape, bf16)] * 2,
        in_specs=[scalars()] + [whole()] * (tp_count + 2),
        out_specs=[whole()] * (tp_count + 2),
        scratch_shapes=[
            pltpu.VMEM((PER_KV, resp, HEAD_DIM), bf16),
            pltpu.VMEM((PER_KV, resp, HEAD_DIM), bf16),
            pltpu.VMEM((total, HEAD_DIM), bf16),
            pltpu.VMEM((total, HEAD_DIM), bf16),
            pltpu.VMEM((HEAD_DIM, total), bf16),
            pltpu.VMEM((resp, resp), f32),
            pltpu.VMEM((total, resp), f32),
            pltpu.VMEM((total, resp), f32),
            pltpu.VMEM((total, resp), bf16),
            pltpu.VMEM((total, resp), bf16),
            pltpu.VMEM((total, HEAD_DIM), f32),
            pltpu.VMEM((total, HEAD_DIM), f32),
        ],
        compiler_params=pltpu.CompilerParams(vmem_limit_bytes=VMEM_LIMIT),
        cost_estimate=pl.CostEstimate(
            flops=flops, bytes_accessed=6 * 1024 * 1024, transcendentals=flops // 1280
        ),
        name="attend",
    )(meta, *packs, own, other)
    return results[:tp_count], results[tp_count], results[tp_count + 1]


def pick(which, choices):
    chosen = choices[0]
    for offset in range(1, len(choices)):
        chosen = jnp.where(which == offset, choices[offset], chosen)
    return chosen


def shards(
    resp_queries, resp_keys, resp_values, resp_dout, prompt_kv, lengths, owners, visible_tiles
):
    tp_count = lax.axis_size("tp")
    section = lax.axis_index("section").astype(jnp.int32)
    rows = resp_queries.shape[0]
    half = prompt_kv.shape[2] // 2
    k_cols = prompt_kv.shape[3]
    k_part = k_cols // CHUNKS
    q_part = k_part * PER_KV
    bf16 = jnp.bfloat16

    owner = owners[0]
    sibling_owner = shifted(owners, "section", 1)[0]
    meta = jnp.concatenate(
        [lax.axis_index("tp").astype(jnp.int32)[None], section[None], lengths, visible_tiles[0]]
    )
    own_half = lax.dynamic_slice_in_dim(prompt_kv[0], section * half, half, 1)
    halves = [own_half[:, :, c * k_part : (c + 1) * k_part] for c in range(CHUNKS)]
    offers = [
        [part] + [shifted(part, "group", offset) for offset in range(1, WIN)] for part in halves
    ]

    packs = pl.pallas_call(
        functools.partial(pack_kernel, tp_count),
        out_shape=[jax.ShapeDtypeStruct((rows, 2 * q_part + 2 * k_part), bf16)]
        * (CHUNKS * tp_count),
        in_specs=[scalars()] + [whole()] * 4,
        out_specs=[whole()] * (CHUNKS * tp_count),
        compiler_params=pltpu.CompilerParams(vmem_limit_bytes=VMEM_LIMIT),
        name="pack",
    )(meta, resp_queries, resp_dout, resp_keys, resp_values)

    returned, kept_grads, shares = [], [], []
    for c in range(CHUNKS):
        mine = packs[c * tp_count : (c + 1) * tp_count]
        inputs = [mine[0]] + [shifted(mine[d], "tp", d) for d in range(1, tp_count)]
        other = shifted(pick(sibling_owner, offers[c]), "section", 1)
        own = pick(owner, offers[c])
        backs, own_grad, other_grad = attend(meta, inputs, own, other)
        sibling_grad = shifted(other_grad, "section", 1)
        terms = []
        for offset in range(WIN):
            term = jnp.where(owner == offset, own_grad.astype(jnp.float32), 0.0) + jnp.where(
                sibling_owner == offset, sibling_grad.astype(jnp.float32), 0.0
            )
            terms.append(term)
        arrived = [terms[0]] + [
            shifted(terms[offset].astype(bf16), "group", -offset).astype(jnp.float32)
            for offset in range(1, WIN)
        ]
        shares.append(functools.reduce(jnp.add, arrived).astype(bf16))
        returned += [backs[0]] + [shifted(backs[d], "tp", -d) for d in range(1, tp_count)]

    grads = pl.pallas_call(
        functools.partial(unpack_kernel, tp_count),
        out_shape=[
            jax.ShapeDtypeStruct(resp_queries.shape, bf16),
            jax.ShapeDtypeStruct(resp_keys.shape, bf16),
            jax.ShapeDtypeStruct(resp_values.shape, bf16),
        ],
        in_specs=[scalars()] + [whole()] * (CHUNKS * tp_count),
        out_specs=[whole()] * 3,
        compiler_params=pltpu.CompilerParams(vmem_limit_bytes=VMEM_LIMIT),
        name="unpack",
    )(meta, *returned)
    return (grads[0], grads[1], grads[2], jnp.concatenate(shares, -1)[None])


def solution(mesh):
    placed = (
        P(("section", "group", "tp"), None),
        P(("section", "group", "tp"), None),
        P(("section", "group", "tp"), None),
        P(("section", "group", "tp"), None),
        P("group", None, None, "tp"),
        P(("section", "group")),
        P(("section", "group")),
        P(("section", "group"), None),
    )
    return jax.shard_map(
        shards,
        mesh=mesh,
        in_specs=placed,
        out_specs=(
            P(("section", "group", "tp"), None),
            P(("section", "group", "tp"), None),
            P(("section", "group", "tp"), None),
            P("group", None, "section", "tp"),
        ),
        check_vma=False,
    )
```

time: 399 us -> 153 us (0.38)
  the two profiles are of different devices: /device:TPU:104 before, /device:TPU:72 now
where the time goes in v1:
time: 153 us
  waiting for transfers between devices  99.3 us (65%)
  starting transfers between devices  26.7 us (17%)
  Pallas kernels  17.2 us (11%)
  between operations  4.84 us (3%)
  other arithmetic  2.92 us (2%)
  local copies, waits for them, and re-layouts  1.85 us (1%)
    ppermute x15, waiting for transfers between devices, shifted(): return lax.ppermute(block, axis, route)  99.3 us
    ppermute x15, starting transfers between devices, shifted(): return lax.ppermute(block, axis, route)  26.7 us
    pallas_call x1, Pallas kernels, attend(): pl.pallas_call(functools.partial(attend_kernel, tp_count, kv_heads), out_...  15 us
  transfers between devices with their start and end apart: 15, of which 10 were waited for; matrix products, arithmetic and copies ran while one was open for 0% of the time, Pallas kernels for 1%

profile of v1, /device:TPU:72, one launch (start us, length us, event | category | flops | bytes accessed | tf_op | source)
XLA Modules:
  0.0 152.9 jit_solution(11829204559388329691)
XLA Ops:
  0.6 0.0 copy-start.4
  0.6 1.2 dynamic-slice_bitcast_fusion
  1.8 1.7 %collective-permute-start.5 = (bf16[2,512,256]{2,1,0:T(8,128)(2,1)S(1)}, bf16[2,512,256]{2,1,0:T(8,128)(2,1)S(1)}, u32[]{:S(2)}, u32[]{:S(2)}) collective-permute-start(bf16[2,512,256]{2,1,0:T(8,128)(2,1)S(1)} %dynamic-slice_bitcast_fusion), channel_id=1, source_target_pairs={{124,0},{0,4},{4,8},{8,12},{12,16},{16,20},{20,24},{24,28},{28,32}... | collective-permute-start | bytes 1572872 | tf_op jit(solution)/shard_map/ppermute | solution.py:29
  3.5 2.3 %collective-permute-start.4 = (bf16[2,512,256]{2,1,0:T(8,128)(2,1)S(1)}, bf16[2,512,256]{2,1,0:T(8,128)(2,1)S(1)}, u32[]{:S(2)}, u32[]{:S(2)}) collective-permute-start(bf16[2,512,256]{2,1,0:T(8,128)(2,1)S(1)} %dynamic-slice_bitcast_fusion), channel_id=1, source_target_pairs={{120,0},{124,4},{0,8},{4,12},{8,16},{12,20},{16,24},{20,28},{24,32... | collective-permute-start | bytes 1572872 | tf_op jit(solution)/shard_map/ppermute | solution.py:29
  5.8 2.4 %collective-permute-start.3 = (bf16[2,512,256]{2,1,0:T(8,128)(2,1)S(1)}, bf16[2,512,256]{2,1,0:T(8,128)(2,1)S(1)}, u32[]{:S(2)}, u32[]{:S(2)}) collective-permute-start(bf16[2,512,256]{2,1,0:T(8,128)(2,1)S(1)} %dynamic-slice_bitcast_fusion), channel_id=1, source_target_pairs={{116,0},{120,4},{124,8},{0,12},{4,16},{8,20},{12,24},{16,28},{20,3... | collective-permute-start | bytes 1572872 | tf_op jit(solution)/shard_map/ppermute | solution.py:29
  8.2 0.0 collective-permute-start.6
  8.8 0.6 collective-permute-done.6
  11.5 5.2 %collective-permute-done.5 = bf16[2,512,256]{2,1,0:T(8,128)(2,1)S(1)} collective-permute-done((bf16[2,512,256]{2,1,0:T(8,128)(2,1)S(1)}, bf16[2,512,256]{2,1,0:T(8,128)(2,1)S(1)}, u32[]{:S(2)}, u32[]{:S(2)}) %collective-permute-start.5) | collective-permute-done | bytes 524320 | tf_op jit(solution)/shard_map/ppermute | solution.py:29
  16.7 29.6 %collective-permute-done.4 = bf16[2,512,256]{2,1,0:T(8,128)(2,1)S(1)} collective-permute-done((bf16[2,512,256]{2,1,0:T(8,128)(2,1)S(1)}, bf16[2,512,256]{2,1,0:T(8,128)(2,1)S(1)}, u32[]{:S(2)}, u32[]{:S(2)}) %collective-permute-start.4) | collective-permute-done | bytes 524320 | tf_op jit(solution)/shard_map/ppermute | solution.py:29
  46.3 0.0 collective-permute-done.3
  46.3 0.0 copy-done.4
  46.3 0.0 copy-start.1
  46.3 0.0 copy-start.2
  46.3 0.0 copy-start.3
  46.3 1.2 select_select_fusion
  47.5 0.0 collective-permute-start.7
  48.2 0.0 copy-start.5
  48.2 0.6 copy-done.5
  48.8 0.1 pad_add_fusion.meta
  48.9 0.0 copy-done
  48.9 0.0 copy-done.1
  48.9 0.0 copy-done.2
  48.9 0.7 pack.1
  49.6 1.6 %collective-permute-start = (bf16[64,3072]{1,0:T(8,128)(2,1)S(1)}, bf16[64,3072]{1,0:T(8,128)(2,1)S(1)}, u32[]{:S(2)}, u32[]{:S(2)}) collective-permute-start(bf16[64,3072]{1,0:T(8,128)(2,1)S(1)} %get-tuple-element.18), channel_id=1, source_target_pairs={{3,0},{0,1},{1,2},{2,3},{7,4},{4,5},{5,6},{6,7},{11,8},{8,9},{9,10... | collective-permute-start | bytes 1179656 | tf_op jit(solution)/shard_map/ppermute | solution.py:29
  51.2 2.7 %collective-permute-start.1 = (bf16[64,3072]{1,0:T(8,128)(2,1)S(1)}, bf16[64,3072]{1,0:T(8,128)(2,1)S(1)}, u32[]{:S(2)}, u32[]{:S(2)}) collective-permute-start(bf16[64,3072]{1,0:T(8,128)(2,1)S(1)} %get-tuple-element.19), channel_id=1, source_target_pairs={{2,0},{3,1},{0,2},{1,3},{6,4},{7,5},{4,6},{5,7},{10,8},{11,9},{8,1... | collective-permute-start | bytes 1179656 | tf_op jit(solution)/shard_map/ppermute | solution.py:29
  53.9 1.4 collective-permute-start.2
  55.3 7.1 %collective-permute-done.refs_1_ = bf16[64,3072]{1,0:T(8,128)(2,1)S(1)} collective-permute-done((bf16[64,3072]{1,0:T(8,128)(2,1)S(1)}, bf16[64,3072]{1,0:T(8,128)(2,1)S(1)}, u32[]{:S(2)}, u32[]{:S(2)}) %collective-permute-start) | collective-permute-done | bytes 393248 | tf_op jit(solution)/shard_map/ppermute | solution.py:29
  62.4 9.4 %collective-permute-done.1.refs_2_ = bf16[64,3072]{1,0:T(8,128)(2,1)S(1)} collective-permute-done((bf16[64,3072]{1,0:T(8,128)(2,1)S(1)}, bf16[64,3072]{1,0:T(8,128)(2,1)S(1)}, u32[]{:S(2)}, u32[]{:S(2)}) %collective-permute-start.1) | collective-permute-done | bytes 393248 | tf_op jit(solution)/shard_map/ppermute | solution.py:29
  71.8 0.0 collective-permute-done.2.refs_3_
  71.8 0.0 collective-permute-done.7.refs_5_
  71.8 15.0 %attend.1 = (bf16[64,1792]{1,0:T(8,128)(2,1)S(1)}, bf16[64,1792]{1,0:T(8,128)(2,1)S(1)}, bf16[64,1792]{1,0:T(8,128)(2,1)S(1)}, bf16[64,1792]{1,0:T(8,128)(2,1)S(...) custom-call(s32[11]{0:T(128)S(1)} %pad_add_fusion.meta, ...), custom_call_target="tpu_custom_call" | custom-call | flops 4194304000 | bytes 6291456 | tf_op jit(solution)/shard_map/attend/pallas_call | solution.py:210
  86.9 0.1 collective-permute-start.11
  87.0 1.9 %collective-permute-done.11 = bf16[2,512,256]{2,1,0:T(8,128)(2,1)S(1)} collective-permute-done((bf16[2,512,256]{2,1,0:T(8,128)(2,1)S(1)}, bf16[2,512,256]{2,1,0:T(8,128)(2,1)S(1)}, u32[]{:S(2)}, u32[]{:S(2)}) %collective-permute-start.11) | collective-permute-done | bytes 524320 | tf_op jit(solution)/shard_map/ppermute | solution.py:29
  88.9 0.5 fusion.6
  89.3 0.1 collective-permute-start.12
  89.4 10.9 %collective-permute-start.13 = (bf16[2,512,256]{2,1,0:T(8,128)(2,1)S(1)}, bf16[2,512,256]{2,1,0:T(8,128)(2,1)S(1)}, u32[]{:S(2)}, u32[]{:S(2)}) collective-permute-start(bf16[2,512,256]{2,1,0:T(8,128)(2,1)S(1)} %get-tuple-element.33), channel_id=1, source_target_pairs={{8,0},{12,4},{16,8},{20,12},{24,16},{28,20},{32,24},{36,28},{40,32... | collective-permute-start | bytes 1572872 | tf_op jit(solution)/shard_map/ppermute | solution.py:29
  100.3 0.1 collective-permute-start.14
  100.4 2.3 %collective-permute-start.8 = (bf16[64,1792]{1,0:T(8,128)(2,1)S(1)}, bf16[64,1792]{1,0:T(8,128)(2,1)S(1)}, u32[]{:S(2)}, u32[]{:S(2)}) collective-permute-start(bf16[64,1792]{1,0:T(8,128)(2,1)S(1)} %get-tuple-element.22), channel_id=1, source_target_pairs={{1,0},{2,1},{3,2},{0,3},{5,4},{6,5},{7,6},{4,7},{9,8},{10,9},{11,1... | collective-permute-start | bytes 688136 | tf_op jit(solution)/shard_map/ppermute | solution.py:29
  102.7 1.1 collective-permute-start.9
  103.8 8.3 %collective-permute-done.8.refs_1_ = bf16[64,1792]{1,0:T(8,128)(2,1)S(1)} collective-permute-done((bf16[64,1792]{1,0:T(8,128)(2,1)S(1)}, bf16[64,1792]{1,0:T(8,128)(2,1)S(1)}, u32[]{:S(2)}, u32[]{:S(2)}) %collective-permute-start.8) | collective-permute-done | bytes 229408 | tf_op jit(solution)/shard_map/ppermute | solution.py:29
  112.1 0.0 collective-permute-start.10
  112.8 0.0 collective-permute-done.9.refs_2_
  112.8 6.9 %collective-permute-done.10.refs_3_ = bf16[64,1792]{1,0:T(8,128)(2,1)S(1)} collective-permute-done((bf16[64,1792]{1,0:T(8,128)(2,1)S(1)}, bf16[64,1792]{1,0:T(8,128)(2,1)S(1)}, u32[]{:S(2)}, u32[]{:S(2)}) %collective-permute-start.10) | collective-permute-done | bytes 229408 | tf_op jit(solution)/shard_map/ppermute | solution.py:29
  119.8 1.5 unpack.1
  121.3 0.0 collective-permute-done.12
  121.3 2.6 %collective-permute-done.13 = bf16[2,512,256]{2,1,0:T(8,128)(2,1)S(1)} collective-permute-done((bf16[2,512,256]{2,1,0:T(8,128)(2,1)S(1)}, bf16[2,512,256]{2,1,0:T(8,128)(2,1)S(1)}, u32[]{:S(2)}, u32[]{:S(2)}) %collective-permute-start.13) | collective-permute-done | bytes 524320 | tf_op jit(solution)/shard_map/ppermute | solution.py:29
  124.0 27.7 %collective-permute-done.14 = bf16[2,512,256]{2,1,0:T(8,128)(2,1)S(1)} collective-permute-done((bf16[2,512,256]{2,1,0:T(8,128)(2,1)S(1)}, bf16[2,512,256]{2,1,0:T(8,128)(2,1)S(1)}, u32[]{:S(2)}, u32[]{:S(2)}) %collective-permute-start.14) | collective-permute-done | bytes 524320 | tf_op jit(solution)/shard_map/ppermute | solution.py:29
  151.6 1.2 fusion.11
  (2 shorter events, 0.0 us)
Async XLA Ops:
  0.6 45.6 %copy-start.4 = (bf16[1,2,1024,256]{3,2,1,0:T(8,128)(2,1)S(1)}, bf16[1,2,1024,256]{3,2,1,0:T(8,128)(2,1)}, u32[]{:S(2)}) copy-start(bf16[1,2,1024,256]{3,2,1,0:T(8,128)(2,1)} %param.12) | copy-start | bytes 3145732
  1.8 14.9 %collective-permute-start.5 = (bf16[2,512,256]{2,1,0:T(8,128)(2,1)S(1)}, bf16[2,512,256]{2,1,0:T(8,128)(2,1)S(1)}, u32[]{:S(2)}, u32[]{:S(2)}) collective-permute-start(bf16[2,512,256]{2,1,0:T(8,128)(2,1)S(1)} %dynamic-slice_bitcast_fusion), channel_id=1, source_target_pairs={{124,0},{0,4},{4,8},{8,12},{12,16},{16,20},{20,24},{24,28},{28,32}... | collective-permute-start | bytes 1572872 | tf_op jit(solution)/shard_map/ppermute | solution.py:29
  3.5 42.8 %collective-permute-start.4 = (bf16[2,512,256]{2,1,0:T(8,128)(2,1)S(1)}, bf16[2,512,256]{2,1,0:T(8,128)(2,1)S(1)}, u32[]{:S(2)}, u32[]{:S(2)}) collective-permute-start(bf16[2,512,256]{2,1,0:T(8,128)(2,1)S(1)} %dynamic-slice_bitcast_fusion), channel_id=1, source_target_pairs={{120,0},{124,4},{0,8},{4,12},{8,16},{12,20},{16,24},{20,28},{24,32... | collective-permute-start | bytes 1572872 | tf_op jit(solution)/shard_map/ppermute | solution.py:29
  5.8 40.5 %collective-permute-start.3 = (bf16[2,512,256]{2,1,0:T(8,128)(2,1)S(1)}, bf16[2,512,256]{2,1,0:T(8,128)(2,1)S(1)}, u32[]{:S(2)}, u32[]{:S(2)}) collective-permute-start(bf16[2,512,256]{2,1,0:T(8,128)(2,1)S(1)} %dynamic-slice_bitcast_fusion), channel_id=1, source_target_pairs={{116,0},{120,4},{124,8},{0,12},{4,16},{8,20},{12,24},{16,28},{20,3... | collective-permute-start | bytes 1572872 | tf_op jit(solution)/shard_map/ppermute | solution.py:29
  8.2 1.2 collective-permute-start.6
  46.3 2.6 %copy-start = (bf16[64,5120]{1,0:T(8,128)(2,1)S(1)}, bf16[64,5120]{1,0:T(8,128)(2,1)}, u32[]{:S(2)}) copy-start(bf16[64,5120]{1,0:T(8,128)(2,1)} %queries.1) | copy-start | bytes 1966084
  46.3 2.6 %copy-start.1 = (bf16[64,5120]{1,0:T(8,128)(2,1)S(1)}, bf16[64,5120]{1,0:T(8,128)(2,1)}, u32[]{:S(2)}) copy-start(bf16[64,5120]{1,0:T(8,128)(2,1)} %grad_out.1) | copy-start | bytes 1966084
  46.3 2.6 %copy-start.2 = (bf16[64,1024]{1,0:T(8,128)(2,1)S(1)}, bf16[64,1024]{1,0:T(8,128)(2,1)}, u32[]{:S(2)}) copy-start(bf16[64,1024]{1,0:T(8,128)(2,1)} %keys.1) | copy-start | bytes 393220
  46.3 2.6 %copy-start.3 = (bf16[64,1024]{1,0:T(8,128)(2,1)S(1)}, bf16[64,1024]{1,0:T(8,128)(2,1)}, u32[]{:S(2)}) copy-start(bf16[64,1024]{1,0:T(8,128)(2,1)} %values.1) | copy-start | bytes 393220
  47.5 24.3 %collective-permute-start.7 = (bf16[2,512,256]{2,1,0:T(8,128)(2,1)}, bf16[2,512,256]{2,1,0:T(8,128)(2,1)S(1)}, u32[]{:S(2)}, u32[]{:S(2)}) collective-permute-start(bf16[2,512,256]{2,1,0:T(8,128)(2,1)} %get-tuple-element.30), channel_id=1, source_target_pairs={{128,0},{0,128},{129,1},{1,129},{130,2},{2,130},{131,3},{3,131},{1... | collective-permute-start | bytes 1572872 | tf_op jit(solution)/shard_map/ppermute | solution.py:29
  48.2 0.7 copy-start.5
  49.6 12.8 %collective-permute-start = (bf16[64,3072]{1,0:T(8,128)(2,1)S(1)}, bf16[64,3072]{1,0:T(8,128)(2,1)S(1)}, u32[]{:S(2)}, u32[]{:S(2)}) collective-permute-start(bf16[64,3072]{1,0:T(8,128)(2,1)S(1)} %get-tuple-element.18), channel_id=1, source_target_pairs={{3,0},{0,1},{1,2},{2,3},{7,4},{4,5},{5,6},{6,7},{11,8},{8,9},{9,10... | collective-permute-start | bytes 1179656 | tf_op jit(solution)/shard_map/ppermute | solution.py:29
  51.2 20.7 %collective-permute-start.1 = (bf16[64,3072]{1,0:T(8,128)(2,1)S(1)}, bf16[64,3072]{1,0:T(8,128)(2,1)S(1)}, u32[]{:S(2)}, u32[]{:S(2)}) collective-permute-start(bf16[64,3072]{1,0:T(8,128)(2,1)S(1)} %get-tuple-element.19), channel_id=1, source_target_pairs={{2,0},{3,1},{0,2},{1,3},{6,4},{7,5},{4,6},{5,7},{10,8},{11,9},{8,1... | collective-permute-start | bytes 1179656 | tf_op jit(solution)/shard_map/ppermute | solution.py:29
  53.9 17.9 %collective-permute-start.2 = (bf16[64,3072]{1,0:T(8,128)(2,1)S(1)}, bf16[64,3072]{1,0:T(8,128)(2,1)S(1)}, u32[]{:S(2)}, u32[]{:S(2)}) collective-permute-start(bf16[64,3072]{1,0:T(8,128)(2,1)S(1)} %get-tuple-element.20), channel_id=1, source_target_pairs={{1,0},{2,1},{3,2},{0,3},{5,4},{6,5},{7,6},{4,7},{9,8},{10,9},{11,1... | collective-permute-start | bytes 1179656 | tf_op jit(solution)/shard_map/ppermute | solution.py:29
  86.9 2.0 %collective-permute-start.11 = (bf16[2,512,256]{2,1,0:T(8,128)(2,1)S(1)}, bf16[2,512,256]{2,1,0:T(8,128)(2,1)S(1)}, u32[]{:S(2)}, u32[]{:S(2)}) collective-permute-start(bf16[2,512,256]{2,1,0:T(8,128)(2,1)S(1)} %get-tuple-element.29), channel_id=1, source_target_pairs={{128,0},{0,128},{129,1},{1,129},{130,2},{2,130},{131,3},{3,131},{1... | collective-permute-start | bytes 1572872 | tf_op jit(solution)/shard_map/ppermute | solution.py:29
  89.3 32.0 %collective-permute-start.12 = (bf16[2,512,256]{2,1,0:T(8,128)(2,1)S(1)}, bf16[2,512,256]{2,1,0:T(8,128)(2,1)S(1)}, u32[]{:S(2)}, u32[]{:S(2)}) collective-permute-start(bf16[2,512,256]{2,1,0:T(8,128)(2,1)S(1)} %get-tuple-element.32), channel_id=1, source_target_pairs={{4,0},{8,4},{12,8},{16,12},{20,16},{24,20},{28,24},{32,28},{36,32}... | collective-permute-start | bytes 1572872 | tf_op jit(solution)/shard_map/ppermute | solution.py:29
  89.4 34.5 %collective-permute-start.13 = (bf16[2,512,256]{2,1,0:T(8,128)(2,1)S(1)}, bf16[2,512,256]{2,1,0:T(8,128)(2,1)S(1)}, u32[]{:S(2)}, u32[]{:S(2)}) collective-permute-start(bf16[2,512,256]{2,1,0:T(8,128)(2,1)S(1)} %get-tuple-element.33), channel_id=1, source_target_pairs={{8,0},{12,4},{16,8},{20,12},{24,16},{28,20},{32,24},{36,28},{40,32... | collective-permute-start | bytes 1572872 | tf_op jit(solution)/shard_map/ppermute | solution.py:29
  100.3 51.3 %collective-permute-start.14 = (bf16[2,512,256]{2,1,0:T(8,128)(2,1)S(1)}, bf16[2,512,256]{2,1,0:T(8,128)(2,1)S(1)}, u32[]{:S(2)}, u32[]{:S(2)}) collective-permute-start(bf16[2,512,256]{2,1,0:T(8,128)(2,1)S(1)} %get-tuple-element.34), channel_id=1, source_target_pairs={{12,0},{16,4},{20,8},{24,12},{28,16},{32,20},{36,24},{40,28},{44,3... | collective-permute-start | bytes 1572872 | tf_op jit(solution)/shard_map/ppermute | solution.py:29
  100.4 11.7 %collective-permute-start.8 = (bf16[64,1792]{1,0:T(8,128)(2,1)S(1)}, bf16[64,1792]{1,0:T(8,128)(2,1)S(1)}, u32[]{:S(2)}, u32[]{:S(2)}) collective-permute-start(bf16[64,1792]{1,0:T(8,128)(2,1)S(1)} %get-tuple-element.22), channel_id=1, source_target_pairs={{1,0},{2,1},{3,2},{0,3},{5,4},{6,5},{7,6},{4,7},{9,8},{10,9},{11,1... | collective-permute-start | bytes 688136 | tf_op jit(solution)/shard_map/ppermute | solution.py:29
  102.7 10.2 %collective-permute-start.9 = (bf16[64,1792]{1,0:T(8,128)(2,1)S(1)}, bf16[64,1792]{1,0:T(8,128)(2,1)S(1)}, u32[]{:S(2)}, u32[]{:S(2)}) collective-permute-start(bf16[64,1792]{1,0:T(8,128)(2,1)S(1)} %get-tuple-element.23), channel_id=1, source_target_pairs={{2,0},{3,1},{0,2},{1,3},{6,4},{7,5},{4,6},{5,7},{10,8},{11,9},{8,1... | collective-permute-start | bytes 688136 | tf_op jit(solution)/shard_map/ppermute | solution.py:29
  112.1 7.7 %collective-permute-start.10 = (bf16[64,1792]{1,0:T(8,128)(2,1)S(1)}, bf16[64,1792]{1,0:T(8,128)(2,1)S(1)}, u32[]{:S(2)}, u32[]{:S(2)}) collective-permute-start(bf16[64,1792]{1,0:T(8,128)(2,1)S(1)} %get-tuple-element.24), channel_id=1, source_target_pairs={{3,0},{0,1},{1,2},{2,3},{7,4},{4,5},{5,6},{6,7},{11,8},{8,9},{9,10... | collective-permute-start | bytes 688136 | tf_op jit(solution)/shard_map/ppermute | solution.py:29

commit v2 on v1

--- a/solution.py
+++ b/solution.py
@@ -13,7 +13,8 @@
 PTILE = 128
 WIN = 4
 PER_KV = HEADS // KV_HEADS
-CHUNKS = 1
+CHUNKS = 2
+ROW = 4
 
 MASKED = -1e30
 SCALING = HEAD_DIM ** (-0.5)
@@ -41,16 +42,18 @@
     q_cols = queries.shape[1] // tp_count
     k_cols = keys.shape[1] // tp_count
     q_part, k_part = q_cols // CHUNKS, k_cols // CHUNKS
-    for chunk in range(CHUNKS):
-        for d in range(tp_count):
-            owner = lax.rem(meta[TP] + d, tp_count)
-            pack = packs[chunk * tp_count + d]
+    for d in range(tp_count):
+        owner = lax.rem(meta[TP] + d, tp_count)
+        pack, at = packs[d], 0
+        for chunk in range(CHUNKS):
             q_at = pl.ds(pl.multiple_of(owner * q_cols + chunk * q_part, 128), q_part)
             k_at = pl.ds(pl.multiple_of(owner * k_cols + chunk * k_part, 128), k_part)
-            pack[:, :q_part] = queries[:, q_at]
-            pack[:, q_part : 2 * q_part] = grad_out[:, q_at]
-            pack[:, 2 * q_part : 2 * q_part + k_part] = keys[:, k_at]
-            pack[:, 2 * q_part + k_part :] = values[:, k_at]
+            pack[:, at : at + q_part] = queries[:, q_at]
+            pack[:, at + q_part : at + 2 * q_part] = grad_out[:, q_at]
+            at += 2 * q_part
+            pack[:, at : at + k_part] = keys[:, k_at]
+            pack[:, at + k_part : at + 2 * k_part] = values[:, k_at]
+            at += 2 * k_part
 
 
 def unpack_kernel(tp_count, meta, *refs):
@@ -58,15 +61,17 @@
     q_cols = grad_q.shape[1] // tp_count
     k_cols = grad_k.shape[1] // tp_count
     q_part, k_part = q_cols // CHUNKS, k_cols // CHUNKS
-    for chunk in range(CHUNKS):
-        for d in range(tp_count):
-            owner = lax.rem(meta[TP] + d, tp_count)
-            pack = packs[chunk * tp_count + d]
+    for d in range(tp_count):
+        owner = lax.rem(meta[TP] + d, tp_count)
+        pack, at = packs[d], 0
+        for chunk in range(CHUNKS):
             q_at = pl.ds(pl.multiple_of(owner * q_cols + chunk * q_part, 128), q_part)
             k_at = pl.ds(pl.multiple_of(owner * k_cols + chunk * k_part, 128), k_part)
-            grad_q[:, q_at] = pack[:, :q_part]
-            grad_k[:, k_at] = pack[:, q_part : q_part + k_part]
-            grad_v[:, k_at] = pack[:, q_part + k_part :]
+            grad_q[:, q_at] = pack[:, at : at + q_part]
+            grad_k[:, k_at] = pack[:, at + q_part : at + q_part + k_part]
+            at += q_part + k_part
+            grad_v[:, k_at] = pack[:, at : at + k_part]
+            at += k_part
 
 
 def place(index, tp, tp_count, rows):
@@ -74,13 +79,14 @@
     return lax.rem(tp - block + tp_count, tp_count) * rows + lax.rem(index, rows)
 
 
-def attend_kernel(tp_count, kv_heads, meta, *refs):
-    packs = refs[:tp_count]
-    own, other = refs[tp_count : tp_count + 2]
-    backs = refs[tp_count + 2 : 2 * tp_count + 2]
-    own_grad, other_grad = refs[2 * tp_count + 2 : 2 * tp_count + 4]
+def attend_kernel(tp_count, kv_heads, chunk, meta, *refs):
+    packs, refs = refs[:tp_count], refs[tp_count:]
+    earlier, refs = refs[: tp_count if chunk else 0], refs[tp_count if chunk else 0 :]
+    (own, other), refs = refs[:2], refs[2:]
+    backs, refs = refs[:tp_count], refs[tp_count:]
+    own_grad, other_grad = refs[:2]
     q_all, do_all, keys, values, keys_t, bias, scores, grad_prob, weights, grad_scores, dk, dv = refs[
-        2 * tp_count + 4 :
+        2:
     ]
     rows = packs[0].shape[0]
     resp = rows * tp_count
@@ -91,6 +97,11 @@
     q_cols = kv_heads * PER_KV * HEAD_DIM
     k_cols = kv_heads * HEAD_DIM
     tp, section, length = meta[TP], meta[SECTION], meta[LENGTH]
+    taken = chunk * 2 * (q_cols + k_cols)
+    given = chunk * (q_cols + 2 * k_cols)
+    if chunk:
+        for d in range(tp_count):
+            backs[d][:, :given] = earlier[d][...]
 
     key_at = place(lax.broadcasted_iota(jnp.int32, (resp, resp), 0), tp, tp_count, rows)
     row_at = place(lax.broadcasted_iota(jnp.int32, (resp, resp), 1), tp, tp_count, rows)
@@ -113,7 +124,7 @@
         values[half:prompt_len] = other[1, :, at]
         for d in range(tp_count):
             pack = packs[d]
-            k_from = 2 * q_cols + kv * HEAD_DIM
+            k_from = taken + 2 * q_cols + kv * HEAD_DIM
             keys[prompt_len + d * rows : prompt_len + (d + 1) * rows] = pack[
                 :, k_from : k_from + HEAD_DIM
             ]
@@ -122,7 +133,7 @@
                 :, v_from : v_from + HEAD_DIM
             ]
             for head in range(PER_KV):
-                q_from = (kv * PER_KV + head) * HEAD_DIM
+                q_from = taken + (kv * PER_KV + head) * HEAD_DIM
                 q_all[head, d * rows : (d + 1) * rows] = pack[:, q_from : q_from + HEAD_DIM]
                 do_all[head, d * rows : (d + 1) * rows] = pack[
                     :, q_cols + q_from : q_cols + q_from + HEAD_DIM
@@ -180,7 +191,7 @@
                 keys_t[...], grad_scores[...], preferred_element_type=jnp.float32
             )
             grad_query = (grad_query_t.T * SCALING).astype(jnp.bfloat16)
-            q_from = (kv * PER_KV + head) * HEAD_DIM
+            q_from = given + (kv * PER_KV + head) * HEAD_DIM
             for d in range(tp_count):
                 backs[d][:, q_from : q_from + HEAD_DIM] = grad_query[d * rows : (d + 1) * rows]
 
@@ -189,7 +200,7 @@
         own_grad[1, :, at] = dv[:half].astype(jnp.bfloat16)
         other_grad[1, :, at] = dv[half:prompt_len].astype(jnp.bfloat16)
         for d in range(tp_count):
-            k_from = q_cols + kv * HEAD_DIM
+            k_from = given + q_cols + kv * HEAD_DIM
             span = slice(prompt_len + d * rows, prompt_len + (d + 1) * rows)
             backs[d][:, k_from : k_from + HEAD_DIM] = (dk[span] * SCALING).astype(jnp.bfloat16)
             backs[d][:, k_from + k_cols : k_from + k_cols + HEAD_DIM] = dv[span].astype(
@@ -197,7 +208,7 @@
             )
 
 
-def attend(meta, packs, own, other):
+def attend(chunk, meta, packs, earlier, own, other):
     tp_count = len(packs)
     rows = packs[0].shape[0]
     resp = rows * tp_count
@@ -208,10 +219,11 @@
     f32, bf16 = jnp.float32, jnp.bfloat16
     flops = 10 * resp * total * kv_heads * PER_KV * HEAD_DIM
     results = pl.pallas_call(
-        functools.partial(attend_kernel, tp_count, kv_heads),
-        out_shape=[jax.ShapeDtypeStruct((rows, q_cols + 2 * k_cols), bf16)] * tp_count
+        functools.partial(attend_kernel, tp_count, kv_heads, chunk),
+        out_shape=[jax.ShapeDtypeStruct((rows, (chunk + 1) * (q_cols + 2 * k_cols)), bf16)]
+        * tp_count
         + [jax.ShapeDtypeStruct(own.shape, bf16)] * 2,
-        in_specs=[scalars()] + [whole()] * (tp_count + 2),
+        in_specs=[scalars()] + [whole()] * (tp_count + len(earlier) + 2),
         out_specs=[whole()] * (tp_count + 2),
         scratch_shapes=[
             pltpu.VMEM((PER_KV, resp, HEAD_DIM), bf16),
@@ -232,7 +244,7 @@
             flops=flops, bytes_accessed=6 * 1024 * 1024, transcendentals=flops // 1280
         ),
         name="attend",
-    )(meta, *packs, own, other)
+    )(meta, *packs, *earlier, own, other)
     return results[:tp_count], results[tp_count], results[tp_count + 1]
 
 
@@ -243,59 +255,87 @@
     return chosen
 
 
+def after(block, earlier):
+    return lax.optimization_barrier((block, earlier))[0]
+
+
+def along_row(block, distance):
+    count = lax.axis_size("group")
+    route = [(i - i % ROW + (i - distance) % ROW, i) for i in range(count)]
+    return lax.ppermute(block, "group", route)
+
+
+def to_row(block, distance):
+    return shifted(block, "group", distance * ROW)
+
+
 def shards(
     resp_queries, resp_keys, resp_values, resp_dout, prompt_kv, lengths, owners, visible_tiles
 ):
     tp_count = lax.axis_size("tp")
     section = lax.axis_index("section").astype(jnp.int32)
+    at_row = lax.rem(lax.axis_index("group").astype(jnp.int32), ROW)
     rows = resp_queries.shape[0]
     half = prompt_kv.shape[2] // 2
     k_cols = prompt_kv.shape[3]
     k_part = k_cols // CHUNKS
     q_part = k_part * PER_KV
-    bf16 = jnp.bfloat16
+    bf16, f32 = jnp.bfloat16, jnp.float32
 
     owner = owners[0]
     sibling_owner = shifted(owners, "section", 1)[0]
     meta = jnp.concatenate(
         [lax.axis_index("tp").astype(jnp.int32)[None], section[None], lengths, visible_tiles[0]]
     )
-    own_half = lax.dynamic_slice_in_dim(prompt_kv[0], section * half, half, 1)
-    halves = [own_half[:, :, c * k_part : (c + 1) * k_part] for c in range(CHUNKS)]
-    offers = [
-        [part] + [shifted(part, "group", offset) for offset in range(1, WIN)] for part in halves
-    ]
-
     packs = pl.pallas_call(
         functools.partial(pack_kernel, tp_count),
-        out_shape=[jax.ShapeDtypeStruct((rows, 2 * q_part + 2 * k_part), bf16)]
-        * (CHUNKS * tp_count),
+        out_shape=[jax.ShapeDtypeStruct((rows, CHUNKS * 2 * (q_part + k_part)), bf16)] * tp_count,
         in_specs=[scalars()] + [whole()] * 4,
-        out_specs=[whole()] * (CHUNKS * tp_count),
+        out_specs=[whole()] * tp_count,
         compiler_params=pltpu.CompilerParams(vmem_limit_bytes=VMEM_LIMIT),
         name="pack",
     )(meta, resp_queries, resp_dout, resp_keys, resp_values)
-
-    returned, kept_grads, shares = [], [], []
+    own_half = lax.dynamic_slice_in_dim(prompt_kv[0], section * half, half, 1)
+    halves = [own_half[:, :, c * k_part : (c + 1) * k_part] for c in range(CHUNKS)]
+    packs, halves = lax.optimization_barrier((packs, halves))
+
+    before = [to_row(part, 1) for part in halves]
+    arrived = [packs[0]] + [shifted(packs[d], "tp", d) for d in range(1, tp_count)]
+    offers = []
     for c in range(CHUNKS):
-        mine = packs[c * tp_count : (c + 1) * tp_count]
-        inputs = [mine[0]] + [shifted(mine[d], "tp", d) for d in range(1, tp_count)]
+        offer = [halves[c]]
+        for offset in range(1, WIN):
+            sent = jnp.where(at_row + offset >= ROW, before[c], halves[c])
+            sent = after(sent, offers[c - 1][offset] if c else arrived[1::2])
+            offer.append(along_row(sent, offset))
+        offers.append(offer)
+
+    backs, shares, passing, held = [], [], [], None
+    for c in range(CHUNKS):
         other = shifted(pick(sibling_owner, offers[c]), "section", 1)
         own = pick(owner, offers[c])
-        backs, own_grad, other_grad = attend(meta, inputs, own, other)
+        if c:
+            own = after(own, held)
+        backs, own_grad, other_grad = attend(c, meta, arrived, backs, own, other)
         sibling_grad = shifted(other_grad, "section", 1)
         terms = []
         for offset in range(WIN):
-            term = jnp.where(owner == offset, own_grad.astype(jnp.float32), 0.0) + jnp.where(
-                sibling_owner == offset, sibling_grad.astype(jnp.float32), 0.0
+            term = jnp.where(owner == offset, own_grad.astype(f32), 0.0) + jnp.where(
+                sibling_owner == offset, sibling_grad.astype(f32), 0.0
             )
-            terms.append(term)
-        arrived = [terms[0]] + [
-            shifted(terms[offset].astype(bf16), "group", -offset).astype(jnp.float32)
-            for offset in range(1, WIN)
-        ]
-        shares.append(functools.reduce(jnp.add, arrived).astype(bf16))
-        returned += [backs[0]] + [shifted(backs[d], "tp", -d) for d in range(1, tp_count)]
+            terms.append(term if offset == 0 else term.astype(bf16))
+        terms = held = lax.optimization_barrier(terms)
+        kept, passed = terms[0], jnp.zeros(terms[0].shape, f32)
+        for offset in range(1, WIN):
+            term = along_row(terms[offset], -offset).astype(f32)
+            crossing = at_row + offset >= ROW
+            kept = kept + jnp.where(crossing, 0.0, term)
+            passed = passed + jnp.where(crossing, term, 0.0)
+        passed = passed.astype(bf16)
+        passing.append(passed)
+        shares.append((kept + to_row(passed, -1).astype(f32)).astype(bf16))
+    backs = after(backs, passing[0])
+    returned = [backs[0]] + [shifted(backs[d], "tp", -d) for d in range(1, tp_count)]
 
     grads = pl.pallas_call(
         functools.partial(unpack_kernel, tp_count),
@@ -304,7 +344,7 @@
             jax.ShapeDtypeStruct(resp_keys.shape, bf16),
             jax.ShapeDtypeStruct(resp_values.shape, bf16),
         ],
-        in_specs=[scalars()] + [whole()] * (CHUNKS * tp_count),
+        in_specs=[scalars()] + [whole()] * tp_count,
         out_specs=[whole()] * 3,
         compiler_params=pltpu.CompilerParams(vmem_limit_bytes=VMEM_LIMIT),
         name="unpack",

time: 153 us -> 103 us (0.67)
  the two profiles are of different devices: /device:TPU:72 before, /device:TPU:96 now
where the time goes in v2:
time: 103 us
  waiting for transfers between devices  47.9 us (47%)
  starting transfers between devices  25.1 us (24%)
  Pallas kernels  18.4 us (18%)
  between operations  4.74 us (5%)
  other arithmetic  4.5 us (4%)
  local copies, waits for them, and re-layouts  2.1 us (2%)
    ppermute x15, waiting for transfers between devices, shifted(): return lax.ppermute(block, axis, route)  30.8 us
    ppermute x12, waiting for transfers between devices, along_row(): return lax.ppermute(block, 'group', route)  17.1 us
    pallas_call x2, Pallas kernels, attend(): pl.pallas_call(functools.partial(attend_kernel, tp_count, kv_heads, chunk...  16.2 us
    ppermute x15, starting transfers between devices, shifted(): return lax.ppermute(block, axis, route)  14.1 us
    ppermute x12, starting transfers between devices, along_row(): return lax.ppermute(block, 'group', route)  11 us
  transfers between devices with their start and end apart: 27, of which 13 were waited for; matrix products, arithmetic and copies ran while one was open for 3% of the time, Pallas kernels for 17%

profile of v2, /device:TPU:96, one launch (start us, length us, event | category | flops | bytes accessed | tf_op | source)
XLA Modules:
  0.0 102.8 jit_solution(13555712448467427900)
XLA Ops:
  1.4 0.5 copy-done
  2.0 0.9 fusion.30
  2.8 0.7 copy-done.6
  3.6 0.7 pack.1
  4.3 3.2 %collective-permute-start.3 = (bf16[2,512,128]{2,1,0:T(8,128)(2,1)}, bf16[2,512,128]{2,1,0:T(8,128)(2,1)}, u32[]{:S(2)}, u32[]{:S(2)}) collective-permute-start(bf16[2,512,128]{2,1,0:T(8,128)(2,1)} %get-tuple-element.56), channel_id=1, source_target_pairs={{112,0},{116,4},{120,8},{124,12},{0,16},{4,20},{8,24},{12,28},{16,... | collective-permute-start | bytes 786440 | tf_op jit(solution)/shard_map/ppermute | solution.py:30
  7.5 1.5 %collective-permute-start = (bf16[64,3072]{1,0:T(8,128)(2,1)S(1)}, bf16[64,3072]{1,0:T(8,128)(2,1)S(1)}, u32[]{:S(2)}, u32[]{:S(2)}) collective-permute-start(bf16[64,3072]{1,0:T(8,128)(2,1)S(1)} %get-tuple-element.53), channel_id=1, source_target_pairs={{3,0},{0,1},{1,2},{2,3},{7,4},{4,5},{5,6},{6,7},{11,8},{8,9},{9,10... | collective-permute-start | bytes 1179656 | tf_op jit(solution)/shard_map/ppermute | solution.py:30
  9.0 1.7 %collective-permute-start.2 = (bf16[64,3072]{1,0:T(8,128)(2,1)S(1)}, bf16[64,3072]{1,0:T(8,128)(2,1)S(1)}, u32[]{:S(2)}, u32[]{:S(2)}) collective-permute-start(bf16[64,3072]{1,0:T(8,128)(2,1)S(1)} %get-tuple-element.55), channel_id=1, source_target_pairs={{1,0},{2,1},{3,2},{0,3},{5,4},{6,5},{7,6},{4,7},{9,8},{10,9},{11,1... | collective-permute-start | bytes 1179656 | tf_op jit(solution)/shard_map/ppermute | solution.py:30
  10.8 2.6 %collective-permute-done.3 = bf16[2,512,128]{2,1,0:T(8,128)(2,1)} collective-permute-done((bf16[2,512,128]{2,1,0:T(8,128)(2,1)}, bf16[2,512,128]{2,1,0:T(8,128)(2,1)}, u32[]{:S(2)}, u32[]{:S(2)}) %collective-permute-start.3) | collective-permute-done | bytes 262176 | tf_op jit(solution)/shard_map/ppermute | solution.py:30
  13.4 1.1 %broadcast_select_fusion.1 = (bf16[2,512,128]{2,1,0:T(8,128)(2,1)S(1)}, bf16[2,512,128]{2,1,0:T(8,128)(2,1)S(1)}, bf16[2,512,128]{2,1,0:T(8,128)(2,1)S(1)}) fusion(bf16[2,512,128]{2,1,0:T(8,128)(2,1)} %collective-permute-done.3, bf16[2,512,128]{2,1,0:T(8,128)(2,1)} %get-tuple-element.56, pred[]{:T(512)S(6)} %ge.8, pred[]{:T(512)S(6)} %ge.7, pred[]{:T(512)S(6)} %ge.6), kind=kLoop, calls=%fused_computation.65 | loop fusion | flops 393216 | bytes 1310723 | tf_op jit(solution)/shard_map/jit(_where)/select_n | solution.py:308
  14.5 4.8 %collective-permute-done.refs_1_ = bf16[64,3072]{1,0:T(8,128)(2,1)S(1)} collective-permute-done((bf16[64,3072]{1,0:T(8,128)(2,1)S(1)}, bf16[64,3072]{1,0:T(8,128)(2,1)S(1)}, u32[]{:S(2)}, u32[]{:S(2)}) %collective-permute-start) | collective-permute-done | bytes 393248 | tf_op jit(solution)/shard_map/ppermute | solution.py:30
  19.3 3.0 %collective-permute-start.4 = (bf16[2,512,128]{2,1,0:T(8,128)(2,1)S(1)}, bf16[2,512,128]{2,1,0:T(8,128)(2,1)S(1)}, u32[]{:S(2)}, u32[]{:S(2)}) collective-permute-start(bf16[2,512,128]{2,1,0:T(8,128)(2,1)S(1)} %get-tuple-element.57), channel_id=1, source_target_pairs={{4,0},{8,4},{12,8},{0,12},{20,16},{24,20},{28,24},{16,28},{36,32},... | collective-permute-start | bytes 786440 | tf_op jit(solution)/shard_map/ppermute | solution.py:265
  22.3 0.6 collective-permute-start.5
  23.0 1.0 collective-permute-start.6
  23.9 1.0 collective-permute-start.9
  25.6 2.8 %collective-permute-start.1 = (bf16[64,3072]{1,0:T(8,128)(2,1)S(1)}, bf16[64,3072]{1,0:T(8,128)(2,1)S(1)}, u32[]{:S(2)}, u32[]{:S(2)}) collective-permute-start(bf16[64,3072]{1,0:T(8,128)(2,1)S(1)} %get-tuple-element.54), channel_id=1, source_target_pairs={{2,0},{3,1},{0,2},{1,3},{6,4},{7,5},{4,6},{5,7},{10,8},{11,9},{8,1... | collective-permute-start | bytes 1179656 | tf_op jit(solution)/shard_map/ppermute | solution.py:30
  30.3 2.0 %collective-permute-done.4 = bf16[2,512,128]{2,1,0:T(8,128)(2,1)S(1)} collective-permute-done((bf16[2,512,128]{2,1,0:T(8,128)(2,1)S(1)}, bf16[2,512,128]{2,1,0:T(8,128)(2,1)S(1)}, u32[]{:S(2)}, u32[]{:S(2)}) %collective-permute-start.4) | collective-permute-done | bytes 262176 | tf_op jit(solution)/shard_map/ppermute | solution.py:265
  32.3 0.8 collective-permute-done.5
  33.1 2.9 %collective-permute-done.6 = bf16[2,512,128]{2,1,0:T(8,128)(2,1)S(1)} collective-permute-done((bf16[2,512,128]{2,1,0:T(8,128)(2,1)S(1)}, bf16[2,512,128]{2,1,0:T(8,128)(2,1)S(1)}, u32[]{:S(2)}, u32[]{:S(2)}) %collective-permute-start.6) | collective-permute-done | bytes 262176 | tf_op jit(solution)/shard_map/ppermute | solution.py:265
  36.0 1.0 %select_select_fusion.2 = (bf16[2,512,128]{2,1,0:T(8,128)(2,1)S(1)}, bf16[2,512,128]{2,1,0:T(8,128)(2,1)S(1)}) fusion(bf16[2,512,128]{2,1,0:T(8,128)(2,1)S(1)} %collective-permute-done.4, bf16[2,512,128]{2,1,0:T(8,128)(2,1)S(1)} %collective-permute-done.5, bf16[2,512,128]{2,1,0:T(8,128)(2,1)S(1)} %collective-permute-done.6, ...), kind=kLoop, calls=%fused_computation.62 | loop fusion | flops 786432 | bytes 1572870 | tf_op jit(solution)/shard_map/jit(_where)/select_n | solution.py:254
  37.2 0.7 collective-permute-start.10
  37.9 0.6 collective-permute-start.11
  38.5 0.8 collective-permute-start.12
  40.0 8.1 %attend.2 = (bf16[64,896]{1,0:T(8,128)(2,1)S(1)}, bf16[64,896]{1,0:T(8,128)(2,1)S(1)}, bf16[64,896]{1,0:T(8,128)(2,1)S(1)}, bf16[64,896]{1,0:T(8,128)(2,1)S(1)},...) custom-call(s32[11]{0:T(128)S(1)} %pad_add_fusion.meta, ...), custom_call_target="tpu_custom_call" | custom-call | flops 2097152000 | bytes 6291456 | tf_op jit(solution)/shard_map/attend/pallas_call | solution.py:221
  48.2 0.4 collective-permute-done.11
  48.6 4.8 %collective-permute-done.12 = bf16[2,512,128]{2,1,0:T(8,128)(2,1)S(1)} collective-permute-done((bf16[2,512,128]{2,1,0:T(8,128)(2,1)S(1)}, bf16[2,512,128]{2,1,0:T(8,128)(2,1)S(1)}, u32[]{:S(2)}, u32[]{:S(2)}) %collective-permute-start.12) | collective-permute-done | bytes 262176 | tf_op jit(solution)/shard_map/ppermute | solution.py:265
  53.7 0.3 fusion.22
  54.0 0.9 collective-permute-start.15
  54.9 0.4 collective-permute-start.16
  55.3 0.8 collective-permute-start.17
  56.1 8.1 %attend.3 = (bf16[64,1792]{1,0:T(8,128)(2,1)S(1)}, bf16[64,1792]{1,0:T(8,128)(2,1)S(1)}, bf16[64,1792]{1,0:T(8,128)(2,1)S(1)}, bf16[64,1792]{1,0:T(8,128)(2,1)S(...) custom-call(s32[11]{0:T(128)S(1)} %pad_add_fusion.meta, ...), custom_call_target="tpu_custom_call" | custom-call | flops 2097152000 | bytes 6291456 | tf_op jit(solution)/shard_map/attend/pallas_call | solution.py:221
  64.3 1.3 %collective-permute-done.16 = bf16[2,512,128]{2,1,0:T(8,128)(2,1)S(1)} collective-permute-done((bf16[2,512,128]{2,1,0:T(8,128)(2,1)S(1)}, bf16[2,512,128]{2,1,0:T(8,128)(2,1)S(1)}, u32[]{:S(2)}, u32[]{:S(2)}) %collective-permute-start.16) | collective-permute-done | bytes 262176 | tf_op jit(solution)/shard_map/ppermute | solution.py:265
  65.6 4.8 %collective-permute-done.17 = bf16[2,512,128]{2,1,0:T(8,128)(2,1)S(1)} collective-permute-done((bf16[2,512,128]{2,1,0:T(8,128)(2,1)S(1)}, bf16[2,512,128]{2,1,0:T(8,128)(2,1)S(1)}, u32[]{:S(2)}, u32[]{:S(2)}) %collective-permute-start.17) | collective-permute-done | bytes 262176 | tf_op jit(solution)/shard_map/ppermute | solution.py:265
  70.4 0.2 fusion.2
  70.6 2.7 %collective-permute-start.18 = (bf16[64,1792]{1,0:T(8,128)(2,1)S(1)}, bf16[64,1792]{1,0:T(8,128)(2,1)S(1)}, u32[]{:S(2)}, u32[]{:S(2)}) collective-permute-start(bf16[64,1792]{1,0:T(8,128)(2,1)S(1)} %get-tuple-element.80), channel_id=1, source_target_pairs={{1,0},{2,1},{3,2},{0,3},{5,4},{6,5},{7,6},{4,7},{9,8},{10,9},{11,1... | collective-permute-start | bytes 688136 | tf_op jit(solution)/shard_map/ppermute | solution.py:30
  73.3 0.3 fusion.29
  73.6 0.7 collective-permute-start.23
  74.3 0.4 collective-permute-start.24
  74.7 1.1 %collective-permute-start.25 = (bf16[2,512,128]{2,1,0:T(8,128)(2,1)S(1)}, bf16[2,512,128]{2,1,0:T(8,128)(2,1)S(1)}, u32[]{:S(2)}, u32[]{:S(2)}) collective-permute-start(bf16[2,512,128]{2,1,0:T(8,128)(2,1)S(1)} %get-tuple-element.91), channel_id=1, source_target_pairs={{12,0},{0,4},{4,8},{8,12},{28,16},{16,20},{20,24},{24,28},{44,32},... | collective-permute-start | bytes 786440 | tf_op jit(solution)/shard_map/ppermute | solution.py:265
  75.7 0.6 collective-permute-start.19
  76.3 7.0 %collective-permute-done.18.refs_1_ = bf16[64,1792]{1,0:T(8,128)(2,1)S(1)} collective-permute-done((bf16[64,1792]{1,0:T(8,128)(2,1)S(1)}, bf16[64,1792]{1,0:T(8,128)(2,1)S(1)}, u32[]{:S(2)}, u32[]{:S(2)}) %collective-permute-start.18) | collective-permute-done | bytes 229408 | tf_op jit(solution)/shard_map/ppermute | solution.py:30
  83.3 0.6 collective-permute-done.19.refs_2_
  83.9 8.0 %collective-permute-done.20.refs_3_ = bf16[64,1792]{1,0:T(8,128)(2,1)S(1)} collective-permute-done((bf16[64,1792]{1,0:T(8,128)(2,1)S(1)}, bf16[64,1792]{1,0:T(8,128)(2,1)S(1)}, u32[]{:S(2)}, u32[]{:S(2)}) %collective-permute-start.20) | collective-permute-done | bytes 229408 | tf_op jit(solution)/shard_map/ppermute | solution.py:30
  91.9 1.6 %unpack.1 = (bf16[64,5120]{1,0:T(8,128)(2,1)}, bf16[64,1024]{1,0:T(8,128)(2,1)}, bf16[64,1024]{1,0:T(8,128)(2,1)}) custom-call(s32[11]{0:T(128)S(1)} %pad_add_fusion.meta, bf16[64,1792]{1,0:T(8,128)(2,1)S(1)} %get-tuple-element.79.refs_0_, bf16[64,1792]{1,0:T(8,128)(2,1)S(1)} %collective-permute-done.18.refs_1_, ...), custom_call_target="tpu_custom_call" | custom-call | tf_op jit(solution)/shard_map/unpack/pallas_call | solution.py:340
  93.5 0.2 fusion.15
  93.8 0.2 fusion.7
  94.0 7.7 %collective-permute-done.26 = bf16[2,512,128]{2,1,0:T(8,128)(2,1)S(1)} collective-permute-done((bf16[2,512,128]{2,1,0:T(8,128)(2,1)S(1)}, bf16[2,512,128]{2,1,0:T(8,128)(2,1)S(1)}, u32[]{:S(2)}, u32[]{:S(2)}) %collective-permute-start.26) | collective-permute-done | bytes 262176 | tf_op jit(solution)/shard_map/ppermute | solution.py:30
  101.7 0.2 fusion.12
  101.9 0.9 maximum_bitcast_fusion
  (38 shorter events, 0.8 us)
Async XLA Ops:
  0.6 1.2 %copy-start = (bf16[1,2,1024,256]{3,2,1,0:T(8,128)(2,1)S(1)}, bf16[1,2,1024,256]{3,2,1,0:T(8,128)(2,1)}, u32[]{:S(2)}) copy-start(bf16[1,2,1024,256]{3,2,1,0:T(8,128)(2,1)} %param.12) | copy-start | bytes 3145732
  1.9 1.7 %copy-start.2 = (bf16[64,5120]{1,0:T(8,128)(2,1)S(1)}, bf16[64,5120]{1,0:T(8,128)(2,1)}, u32[]{:S(2)}) copy-start(bf16[64,5120]{1,0:T(8,128)(2,1)} %grad_out.1) | copy-start | bytes 1966084
  1.9 1.7 %copy-start.1 = (bf16[64,5120]{1,0:T(8,128)(2,1)S(1)}, bf16[64,5120]{1,0:T(8,128)(2,1)}, u32[]{:S(2)}) copy-start(bf16[64,5120]{1,0:T(8,128)(2,1)} %queries.1) | copy-start | bytes 1966084
  1.9 1.6 %copy-start.3 = (bf16[64,1024]{1,0:T(8,128)(2,1)S(1)}, bf16[64,1024]{1,0:T(8,128)(2,1)}, u32[]{:S(2)}) copy-start(bf16[64,1024]{1,0:T(8,128)(2,1)} %keys.1) | copy-start | bytes 393220
  1.9 1.6 %copy-start.4 = (bf16[64,1024]{1,0:T(8,128)(2,1)S(1)}, bf16[64,1024]{1,0:T(8,128)(2,1)}, u32[]{:S(2)}) copy-start(bf16[64,1024]{1,0:T(8,128)(2,1)} %values.1) | copy-start | bytes 393220
  2.8 0.7 copy-start.6
  4.3 9.1 %collective-permute-start.3 = (bf16[2,512,128]{2,1,0:T(8,128)(2,1)}, bf16[2,512,128]{2,1,0:T(8,128)(2,1)}, u32[]{:S(2)}, u32[]{:S(2)}) collective-permute-start(bf16[2,512,128]{2,1,0:T(8,128)(2,1)} %get-tuple-element.56), channel_id=1, source_target_pairs={{112,0},{116,4},{120,8},{124,12},{0,16},{4,20},{8,24},{12,28},{16,... | collective-permute-start | bytes 786440 | tf_op jit(solution)/shard_map/ppermute | solution.py:30
  7.5 11.8 %collective-permute-start = (bf16[64,3072]{1,0:T(8,128)(2,1)S(1)}, bf16[64,3072]{1,0:T(8,128)(2,1)S(1)}, u32[]{:S(2)}, u32[]{:S(2)}) collective-permute-start(bf16[64,3072]{1,0:T(8,128)(2,1)S(1)} %get-tuple-element.53), channel_id=1, source_target_pairs={{3,0},{0,1},{1,2},{2,3},{7,4},{4,5},{5,6},{6,7},{11,8},{8,9},{9,10... | collective-permute-start | bytes 1179656 | tf_op jit(solution)/shard_map/ppermute | solution.py:30
  9.0 10.3 %collective-permute-start.2 = (bf16[64,3072]{1,0:T(8,128)(2,1)S(1)}, bf16[64,3072]{1,0:T(8,128)(2,1)S(1)}, u32[]{:S(2)}, u32[]{:S(2)}) collective-permute-start(bf16[64,3072]{1,0:T(8,128)(2,1)S(1)} %get-tuple-element.55), channel_id=1, source_target_pairs={{1,0},{2,1},{3,2},{0,3},{5,4},{6,5},{7,6},{4,7},{9,8},{10,9},{11,1... | collective-permute-start | bytes 1179656 | tf_op jit(solution)/shard_map/ppermute | solution.py:30
  10.8 13.2 %copy-start.5 = (bf16[2,512,128]{2,1,0:T(8,128)(2,1)S(1)}, bf16[2,512,128]{2,1,0:T(8,128)(2,1)}, u32[]{:S(2)}) copy-start(bf16[2,512,128]{2,1,0:T(8,128)(2,1)} %get-tuple-element.64) | copy-start | bytes 786436
  19.3 13.0 %collective-permute-start.4 = (bf16[2,512,128]{2,1,0:T(8,128)(2,1)S(1)}, bf16[2,512,128]{2,1,0:T(8,128)(2,1)S(1)}, u32[]{:S(2)}, u32[]{:S(2)}) collective-permute-start(bf16[2,512,128]{2,1,0:T(8,128)(2,1)S(1)} %get-tuple-element.57), channel_id=1, source_target_pairs={{4,0},{8,4},{12,8},{0,12},{20,16},{24,20},{28,24},{16,28},{36,32},... | collective-permute-start | bytes 786440 | tf_op jit(solution)/shard_map/ppermute | solution.py:265
  22.3 10.8 %collective-permute-start.5 = (bf16[2,512,128]{2,1,0:T(8,128)(2,1)S(1)}, bf16[2,512,128]{2,1,0:T(8,128)(2,1)S(1)}, u32[]{:S(2)}, u32[]{:S(2)}) collective-permute-start(bf16[2,512,128]{2,1,0:T(8,128)(2,1)S(1)} %get-tuple-element.58), channel_id=1, source_target_pairs={{8,0},{12,4},{0,8},{4,12},{24,16},{28,20},{16,24},{20,28},{40,32},... | collective-permute-start | bytes 786440 | tf_op jit(solution)/shard_map/ppermute | solution.py:265
  23.0 13.1 %collective-permute-start.6 = (bf16[2,512,128]{2,1,0:T(8,128)(2,1)S(1)}, bf16[2,512,128]{2,1,0:T(8,128)(2,1)S(1)}, u32[]{:S(2)}, u32[]{:S(2)}) collective-permute-start(bf16[2,512,128]{2,1,0:T(8,128)(2,1)S(1)} %get-tuple-element.59), channel_id=1, source_target_pairs={{12,0},{0,4},{4,8},{8,12},{28,16},{16,20},{20,24},{24,28},{44,32},... | collective-permute-start | bytes 786440 | tf_op jit(solution)/shard_map/ppermute | solution.py:265
  23.9 1.7 %collective-permute-start.7 = (s32[1]{0:T(128)}, s32[1]{0:T(128)}, u32[]{:S(2)}, u32[]{:S(2)}) collective-permute-start(s32[1]{0:T(128)} %param.14), channel_id=1, source_target_pairs={{128,0},{0,128},{129,1},{1,129},{130,2},{2,130},{131,3},{3,131},{1... | collective-permute-start | bytes 20 | tf_op jit(solution)/shard_map/ppermute | solution.py:30
  23.9 13.2 %collective-permute-start.9 = (bf16[2,512,128]{2,1,0:T(8,128)(2,1)S(1)}, bf16[2,512,128]{2,1,0:T(8,128)(2,1)S(1)}, u32[]{:S(2)}, u32[]{:S(2)}) collective-permute-start(bf16[2,512,128]{2,1,0:T(8,128)(2,1)S(1)} %copy-done.5), channel_id=1, source_target_pairs={{112,0},{116,4},{120,8},{124,12},{0,16},{4,20},{8,24},{12,28},{16,... | collective-permute-start | bytes 786440 | tf_op jit(solution)/shard_map/ppermute | solution.py:30
  25.6 14.4 %collective-permute-start.1 = (bf16[64,3072]{1,0:T(8,128)(2,1)S(1)}, bf16[64,3072]{1,0:T(8,128)(2,1)S(1)}, u32[]{:S(2)}, u32[]{:S(2)}) collective-permute-start(bf16[64,3072]{1,0:T(8,128)(2,1)S(1)} %get-tuple-element.54), channel_id=1, source_target_pairs={{2,0},{3,1},{0,2},{1,3},{6,4},{7,5},{4,6},{5,7},{10,8},{11,9},{8,1... | collective-permute-start | bytes 1179656 | tf_op jit(solution)/shard_map/ppermute | solution.py:30
  37.1 3.0 %collective-permute-start.8 = (bf16[2,512,128]{2,1,0:T(8,128)(2,1)S(1)}, bf16[2,512,128]{2,1,0:T(8,128)(2,1)S(1)}, u32[]{:S(2)}, u32[]{:S(2)}) collective-permute-start(bf16[2,512,128]{2,1,0:T(8,128)(2,1)S(1)} %get-tuple-element.94), channel_id=1, source_target_pairs={{128,0},{0,128},{129,1},{1,129},{130,2},{2,130},{131,3},{3,131},{1... | collective-permute-start | bytes 786440 | tf_op jit(solution)/shard_map/ppermute | solution.py:30
  37.2 11.0 %collective-permute-start.10 = (bf16[2,512,128]{2,1,0:T(8,128)(2,1)S(1)}, bf16[2,512,128]{2,1,0:T(8,128)(2,1)S(1)}, u32[]{:S(2)}, u32[]{:S(2)}) collective-permute-start(bf16[2,512,128]{2,1,0:T(8,128)(2,1)S(1)} %get-tuple-element.65), channel_id=1, source_target_pairs={{4,0},{8,4},{12,8},{0,12},{20,16},{24,20},{28,24},{16,28},{36,32},... | collective-permute-start | bytes 786440 | tf_op jit(solution)/shard_map/ppermute | solution.py:265
  37.9 10.7 %collective-permute-start.11 = (bf16[2,512,128]{2,1,0:T(8,128)(2,1)S(1)}, bf16[2,512,128]{2,1,0:T(8,128)(2,1)S(1)}, u32[]{:S(2)}, u32[]{:S(2)}) collective-permute-start(bf16[2,512,128]{2,1,0:T(8,128)(2,1)S(1)} %get-tuple-element.66), channel_id=1, source_target_pairs={{8,0},{12,4},{0,8},{4,12},{24,16},{28,20},{16,24},{20,28},{40,32},... | collective-permute-start | bytes 786440 | tf_op jit(solution)/shard_map/ppermute | solution.py:265
  38.5 14.9 %collective-permute-start.12 = (bf16[2,512,128]{2,1,0:T(8,128)(2,1)S(1)}, bf16[2,512,128]{2,1,0:T(8,128)(2,1)S(1)}, u32[]{:S(2)}, u32[]{:S(2)}) collective-permute-start(bf16[2,512,128]{2,1,0:T(8,128)(2,1)S(1)} %get-tuple-element.67), channel_id=1, source_target_pairs={{12,0},{0,4},{4,8},{8,12},{28,16},{16,20},{20,24},{24,28},{44,32},... | collective-permute-start | bytes 786440 | tf_op jit(solution)/shard_map/ppermute | solution.py:265
  48.1 5.6 %collective-permute-start.13 = (bf16[2,512,128]{2,1,0:T(8,128)(2,1)S(1)}, bf16[2,512,128]{2,1,0:T(8,128)(2,1)S(1)}, u32[]{:S(2)}, u32[]{:S(2)}) collective-permute-start(bf16[2,512,128]{2,1,0:T(8,128)(2,1)S(1)} %get-tuple-element.69), channel_id=1, source_target_pairs={{128,0},{0,128},{129,1},{1,129},{130,2},{2,130},{131,3},{3,131},{1... | collective-permute-start | bytes 786440 | tf_op jit(solution)/shard_map/ppermute | solution.py:30
  53.5 2.5 %collective-permute-start.14 = (bf16[2,512,128]{2,1,0:T(8,128)(2,1)S(1)}, bf16[2,512,128]{2,1,0:T(8,128)(2,1)S(1)}, u32[]{:S(2)}, u32[]{:S(2)}) collective-permute-start(bf16[2,512,128]{2,1,0:T(8,128)(2,1)S(1)} %get-tuple-element.92), channel_id=1, source_target_pairs={{128,0},{0,128},{129,1},{1,129},{130,2},{2,130},{131,3},{3,131},{1... | collective-permute-start | bytes 786440 | tf_op jit(solution)/shard_map/ppermute | solution.py:30
  54.0 10.3 %collective-permute-start.15 = (bf16[2,512,128]{2,1,0:T(8,128)(2,1)S(1)}, bf16[2,512,128]{2,1,0:T(8,128)(2,1)S(1)}, u32[]{:S(2)}, u32[]{:S(2)}) collective-permute-start(bf16[2,512,128]{2,1,0:T(8,128)(2,1)S(1)} %get-tuple-element.71), channel_id=1, source_target_pairs={{4,0},{8,4},{12,8},{0,12},{20,16},{24,20},{28,24},{16,28},{36,32},... | collective-permute-start | bytes 786440 | tf_op jit(solution)/shard_map/ppermute | solution.py:265
  54.9 10.7 %collective-permute-start.16 = (bf16[2,512,128]{2,1,0:T(8,128)(2,1)S(1)}, bf16[2,512,128]{2,1,0:T(8,128)(2,1)S(1)}, u32[]{:S(2)}, u32[]{:S(2)}) collective-permute-start(bf16[2,512,128]{2,1,0:T(8,128)(2,1)S(1)} %get-tuple-element.72), channel_id=1, source_target_pairs={{8,0},{12,4},{0,8},{4,12},{24,16},{28,20},{16,24},{20,28},{40,32},... | collective-permute-start | bytes 786440 | tf_op jit(solution)/shard_map/ppermute | solution.py:265
  55.3 15.1 %collective-permute-start.17 = (bf16[2,512,128]{2,1,0:T(8,128)(2,1)S(1)}, bf16[2,512,128]{2,1,0:T(8,128)(2,1)S(1)}, u32[]{:S(2)}, u32[]{:S(2)}) collective-permute-start(bf16[2,512,128]{2,1,0:T(8,128)(2,1)S(1)} %get-tuple-element.73), channel_id=1, source_target_pairs={{12,0},{0,4},{4,8},{8,12},{28,16},{16,20},{20,24},{24,28},{44,32},... | collective-permute-start | bytes 786440 | tf_op jit(solution)/shard_map/ppermute | solution.py:265
  64.2 9.1 %collective-permute-start.22 = (bf16[2,512,128]{2,1,0:T(8,128)(2,1)S(1)}, bf16[2,512,128]{2,1,0:T(8,128)(2,1)S(1)}, u32[]{:S(2)}, u32[]{:S(2)}) collective-permute-start(bf16[2,512,128]{2,1,0:T(8,128)(2,1)S(1)} %get-tuple-element.87), channel_id=1, source_target_pairs={{128,0},{0,128},{129,1},{1,129},{130,2},{2,130},{131,3},{3,131},{1... | collective-permute-start | bytes 786440 | tf_op jit(solution)/shard_map/ppermute | solution.py:30
  70.6 12.7 %collective-permute-start.18 = (bf16[64,1792]{1,0:T(8,128)(2,1)S(1)}, bf16[64,1792]{1,0:T(8,128)(2,1)S(1)}, u32[]{:S(2)}, u32[]{:S(2)}) collective-permute-start(bf16[64,1792]{1,0:T(8,128)(2,1)S(1)} %get-tuple-element.80), channel_id=1, source_target_pairs={{1,0},{2,1},{3,2},{0,3},{5,4},{6,5},{7,6},{4,7},{9,8},{10,9},{11,1... | collective-permute-start | bytes 688136 | tf_op jit(solution)/shard_map/ppermute | solution.py:30
  73.6 19.9 %collective-permute-start.23 = (bf16[2,512,128]{2,1,0:T(8,128)(2,1)S(1)}, bf16[2,512,128]{2,1,0:T(8,128)(2,1)S(1)}, u32[]{:S(2)}, u32[]{:S(2)}) collective-permute-start(bf16[2,512,128]{2,1,0:T(8,128)(2,1)S(1)} %get-tuple-element.89), channel_id=1, source_target_pairs={{4,0},{8,4},{12,8},{0,12},{20,16},{24,20},{28,24},{16,28},{36,32},... | collective-permute-start | bytes 786440 | tf_op jit(solution)/shard_map/ppermute | solution.py:265
  74.3 19.2 %collective-permute-start.24 = (bf16[2,512,128]{2,1,0:T(8,128)(2,1)S(1)}, bf16[2,512,128]{2,1,0:T(8,128)(2,1)S(1)}, u32[]{:S(2)}, u32[]{:S(2)}) collective-permute-start(bf16[2,512,128]{2,1,0:T(8,128)(2,1)S(1)} %get-tuple-element.90), channel_id=1, source_target_pairs={{8,0},{12,4},{0,8},{4,12},{24,16},{28,20},{16,24},{20,28},{40,32},... | collective-permute-start | bytes 786440 | tf_op jit(solution)/shard_map/ppermute | solution.py:265
  74.7 18.8 %collective-permute-start.25 = (bf16[2,512,128]{2,1,0:T(8,128)(2,1)S(1)}, bf16[2,512,128]{2,1,0:T(8,128)(2,1)S(1)}, u32[]{:S(2)}, u32[]{:S(2)}) collective-permute-start(bf16[2,512,128]{2,1,0:T(8,128)(2,1)S(1)} %get-tuple-element.91), channel_id=1, source_target_pairs={{12,0},{0,4},{4,8},{8,12},{28,16},{16,20},{20,24},{24,28},{44,32},... | collective-permute-start | bytes 786440 | tf_op jit(solution)/shard_map/ppermute | solution.py:265
  75.7 8.2 %collective-permute-start.19 = (bf16[64,1792]{1,0:T(8,128)(2,1)S(1)}, bf16[64,1792]{1,0:T(8,128)(2,1)S(1)}, u32[]{:S(2)}, u32[]{:S(2)}) collective-permute-start(bf16[64,1792]{1,0:T(8,128)(2,1)S(1)} %get-tuple-element.81), channel_id=1, source_target_pairs={{2,0},{3,1},{0,2},{1,3},{6,4},{7,5},{4,6},{5,7},{10,8},{11,9},{8,1... | collective-permute-start | bytes 688136 | tf_op jit(solution)/shard_map/ppermute | solution.py:30
  83.3 8.6 %collective-permute-start.20 = (bf16[64,1792]{1,0:T(8,128)(2,1)S(1)}, bf16[64,1792]{1,0:T(8,128)(2,1)S(1)}, u32[]{:S(2)}, u32[]{:S(2)}) collective-permute-start(bf16[64,1792]{1,0:T(8,128)(2,1)S(1)} %get-tuple-element.82), channel_id=1, source_target_pairs={{3,0},{0,1},{1,2},{2,3},{7,4},{4,5},{5,6},{6,7},{11,8},{8,9},{9,10... | collective-permute-start | bytes 688136 | tf_op jit(solution)/shard_map/ppermute | solution.py:30
  83.9 9.8 %collective-permute-start.21 = (bf16[2,512,128]{2,1,0:T(8,128)(2,1)S(1)}, bf16[2,512,128]{2,1,0:T(8,128)(2,1)S(1)}, u32[]{:S(2)}, u32[]{:S(2)}) collective-permute-start(bf16[2,512,128]{2,1,0:T(8,128)(2,1)S(1)} %fusion.2), channel_id=1, source_target_pairs={{16,0},{20,4},{24,8},{28,12},{32,16},{36,20},{40,24},{44,28},{48,3... | collective-permute-start | bytes 786440 | tf_op jit(solution)/shard_map/ppermute | solution.py:30
  93.7 8.1 %collective-permute-start.26 = (bf16[2,512,128]{2,1,0:T(8,128)(2,1)S(1)}, bf16[2,512,128]{2,1,0:T(8,128)(2,1)S(1)}, u32[]{:S(2)}, u32[]{:S(2)}) collective-permute-start(bf16[2,512,128]{2,1,0:T(8,128)(2,1)S(1)} %fusion.15), channel_id=1, source_target_pairs={{16,0},{20,4},{24,8},{28,12},{32,16},{36,20},{40,24},{44,28},{48,3... | collective-permute-start | bytes 786440 | tf_op jit(solution)/shard_map/ppermute | solution.py:30
